TPU v7x, 32 devices: a whole 2x2x4 slice. The times are simulated.
32 devices in a mesh: dp: 2 (over y), row: 4 (over z), col: 4 (over x, core).
Axes of the slice: x: 2, y: 2, z: 4, core: 2. Of those that a mesh axis runs over, the one named last changes fastest.
Arguments:
- tokens_in: bfloat16 [8192, 1024], P('dp', ('row', 'col')), may hold values from -6 to 6
- gain_first: float32 [1024], P(('row', 'col')), may hold values from 0.5 to 1.5
- proj_gate: bfloat16 [1024, 1536], P('row', 'col'), may hold values from -0.1875 to 0.1875
- proj_inner: bfloat16 [1024, 1536], P('row', 'col'), may hold values from -0.1875 to 0.1875
- proj_step: bfloat16 [1024, 24], P('row', 'col'), may hold values from -0.1875 to 0.1875
- proj_query: bfloat16 [1024, 512], P('row', 'col'), may hold values from -0.1875 to 0.1875
- proj_state: bfloat16 [1024, 256], P('row'), may hold values from -0.1875 to 0.1875
- proj_keyval: bfloat16 [1024, 256], P('row'), may hold values from -0.1875 to 0.1875
- conv_inner: float32 [4, 1536], P(None, 'col'), may hold values from -3 to 3
- conv_state: float32 [4, 256], replicated, may hold values from -3 to 3
- step_bias: float32 [24], P('col'), may hold values from -3.5 to -0.5
- decay_log: float32 [24], P('col'), may hold values from -5 to 0.5
- skip_scale: float32 [24], P('col'), may hold values from 2 to 20
- mixer_gain: float32 [1536], P('col'), may hold values from 0.5 to 1.5
- out_mamba: bfloat16 [1536, 1024], P('col', 'row'), may hold values from -0.15625 to 0.15625
- out_attn: bfloat16 [512, 1024], P('col', 'row'), may hold values from -1 to 1
- gain_second: float32 [1024], P(('row', 'col')), may hold values from 0.5 to 1.5
- ffn_gate: bfloat16 [1024, 2048], P('row', 'col'), may hold values from -0.1875 to 0.1875
- ffn_up: bfloat16 [1024, 2048], P('row', 'col'), may hold values from -0.1875 to 0.1875
- ffn_down: bfloat16 [2048, 1024], P('col', 'row'), may hold values from -0.125 to 0.125
- out_grad: bfloat16 [8192, 1024], P('dp', ('row', 'col')), may hold values from -6 to 6
Outputs:
- block_out: bfloat16 [8192, 1024], P('dp', ('row', 'col'))
- grad_tokens: bfloat16 [8192, 1024], P('dp', ('row', 'col'))
- grad_gain_first: float32 [1024], P(('row', 'col'))
- grad_proj_gate: float32 [1024, 1536], P('row', 'col')
- grad_proj_inner: float32 [1024, 1536], P('row', 'col')
- grad_proj_step: float32 [1024, 24], P('row', 'col')
- grad_proj_query: float32 [1024, 512], P('row', 'col')
- grad_proj_state: float32 [1024, 256], P('row')
- grad_proj_keyval: float32 [1024, 256], P('row')
- grad_conv_inner: float32 [4, 1536], P(None, 'col')
- grad_conv_state: float32 [4, 256], replicated
- grad_step_bias: float32 [24], P('col')
- grad_decay_log: float32 [24], P('col')
- grad_skip_scale: float32 [24], P('col')
- grad_mixer_gain: float32 [1536], P('col')
- grad_out_mamba: float32 [1536, 1024], P('col', 'row')
- grad_out_attn: float32 [512, 1024], P('col', 'row')
- grad_gain_second: float32 [1024], P(('row', 'col'))
- grad_ffn_gate: float32 [1024, 2048], P('row', 'col')
- grad_ffn_up: float32 [1024, 2048], P('row', 'col')
- grad_ffn_down: float32 [2048, 1024], P('col', 'row')
All inputs are finite; a program needn't handle non-finite values.
Results may differ from a plain program's by a relative error of at most 0.019.
Values may be sent and summed in bfloat16 or wider, within the bound.
A program may use at most 192 MiB of HBM per device.

v0:
```python
import math

import jax
import jax.numpy as jnp
from jax import lax
from jax.sharding import PartitionSpec as P

D = 1024
HQ = 8
HK = 2
HD = 64
DI = 1536
SEQ_LEN = 1024


EPS = 1e-06
HIGH = lax.Precision.HIGHEST


def plain_dot(left, right):
    return jnp.dot(left, right, preferred_element_type=jnp.float32)


def dot_nt(left, right):
    return lax.dot_general(
        left, right, (((1,), (1,)), ((), ())), preferred_element_type=jnp.float32
    )


def dot_tn(left, right):
    return lax.dot_general(
        left, right, (((0,), (0,)), ((), ())), preferred_element_type=jnp.float32
    )


def grid_total(values):
    return lax.psum(values, ("row", "col"))


def head_total(values):
    return lax.psum(values, "col")


def widen(values):
    return lax.all_gather(values, "col", axis=1, tiled=True)


def lengthen(values):
    return lax.all_gather(values, "row", axis=0, tiled=True)


def narrow(partial_sum):
    return lax.psum_scatter(partial_sum, "col", scatter_dimension=1, tiled=True)


def spread(gathered, weight, flipped):

    def term():
        if flipped:
            return dot_nt(gathered, weight)
        return plain_dot(gathered, weight)

    return lax.psum_scatter(term(), "row", scatter_dimension=0, tiled=True)


def norm_apply(values, gain_vec, width_all, total_fn):
    row_scale = lax.rsqrt(total_fn(jnp.sum(values * values, axis=1)) / width_all + EPS)
    return (values * row_scale[:, None] * gain_vec, row_scale)


def norm_back(values, row_scale, gain_vec, grads, width_all, total_fn):
    inner = total_fn(jnp.sum(grads * gain_vec * values, axis=1))
    d_values = (
        grads * gain_vec * row_scale[:, None] - values * (inner * row_scale**3 / width_all)[:, None]
    )
    d_gain = jnp.sum(grads * values * row_scale[:, None], axis=0)
    return (d_values, d_gain)


def causal_conv(signal, kernel):
    tap_count = kernel.shape[0]
    length = signal.shape[0]
    padded = jnp.concatenate(
        [jnp.zeros((tap_count - 1, signal.shape[1]), jnp.float32), signal], axis=0
    )
    result = kernel[tap_count - 1] * signal
    for offset in range(tap_count - 1):
        result = result + kernel[offset] * padded[offset : offset + length]
    return result


def mixer_front(
    inputs, conv_inner, conv_state, step_bias, decay_log, skip_scale, key_pick, head_dim
):
    inner_width = conv_inner.shape[1]
    mamba_heads = step_bias.shape[0]
    state_size = conv_state.shape[1] // 2
    query_width = key_pick.shape[0] * head_dim
    length = inputs.shape[0]
    gate_part = inputs[:, :inner_width]
    inner_part = inputs[:, inner_width : 2 * inner_width]
    first_col = 2 * inner_width
    step_part = inputs[:, first_col : first_col + mamba_heads]
    first_col = first_col + mamba_heads
    query_part = inputs[:, first_col : first_col + query_width]
    first_col = first_col + query_width
    state_part = inputs[:, first_col : first_col + 2 * state_size]
    keyval_part = inputs[:, first_col + 2 * state_size :]
    positions = jnp.arange(length)
    causal = positions[:, None] >= positions[None, :]
    mixed_inner = jax.nn.silu(causal_conv(inner_part, conv_inner))
    mixed_state = jax.nn.silu(causal_conv(state_part, conv_state))
    b_matrix = mixed_state[:, :state_size]
    c_matrix = mixed_state[:, state_size:]
    step_size = jax.nn.softplus(step_part + step_bias)
    decay_sum = jnp.cumsum(step_size * -jnp.exp(decay_log), axis=0)
    spans = decay_sum.T[:, :, None] - decay_sum.T[:, None, :]
    mixing = jnp.where(causal, jnp.exp(jnp.where(causal, spans, 0.0)), 0.0)
    affinity = jnp.dot(c_matrix, b_matrix.T, precision=HIGH)
    heads_inner = mixed_inner.reshape(length, mamba_heads, -1)
    scaled_inner = heads_inner * step_size[:, :, None]
    ssm_out = jnp.einsum("hts,shp->thp", mixing * affinity[None], scaled_inner, precision=HIGH)
    ssm_out = ssm_out + skip_scale[None, :, None] * heads_inner
    gated = ssm_out.reshape(length, inner_width) * jax.nn.silu(gate_part)
    key_heads = keyval_part.shape[1] // (2 * head_dim)
    queries = query_part.reshape(length, -1, head_dim)
    keys_all = keyval_part[:, : key_heads * head_dim].reshape(length, key_heads, head_dim)
    values_all = keyval_part[:, key_heads * head_dim :].reshape(length, key_heads, head_dim)
    keys_used = jnp.take(keys_all, key_pick, axis=1)
    values_used = jnp.take(values_all, key_pick, axis=1)
    scores = jnp.einsum("thd,shd->hts", queries, keys_used, precision=HIGH) / math.sqrt(head_dim)
    scores = jnp.where(causal[None], scores, -1e30)
    peak = jnp.max(scores, axis=2, keepdims=True)
    weights = jnp.exp(scores - peak)
    weights = weights / jnp.sum(weights, axis=2, keepdims=True)
    attended = jnp.einsum("hts,shd->thd", weights, values_used, precision=HIGH).reshape(length, -1)
    return (gated, attended)


def on_device(
    tokens_in,
    gain_first,
    proj_gate,
    proj_inner,
    proj_step,
    proj_query,
    proj_state,
    proj_keyval,
    conv_inner,
    conv_state,
    step_bias,
    decay_log,
    skip_scale,
    mixer_gain,
    out_mamba,
    out_attn,
    gain_second,
    ffn_gate,
    ffn_up,
    ffn_down,
    out_grad,
):
    inner_local = proj_gate.shape[1]
    step_local = proj_step.shape[1]
    query_local = proj_query.shape[1]
    block_cols = 2 * inner_local + step_local + query_local
    state_cols = proj_state.shape[1]
    ffn_local = ffn_gate.shape[1]
    heads_local = query_local // HD
    key_pick = (lax.axis_index("col") * heads_local + jnp.arange(heads_local)) // (HQ // HK)
    kernel_in = jnp.concatenate(
        [proj_gate, proj_inner, proj_step, proj_query, proj_state, proj_keyval], axis=1
    )
    kernel_ffn = jnp.concatenate([ffn_gate, ffn_up], axis=1)
    kernel_out = jnp.concatenate([out_mamba, out_attn], axis=0)
    residual = tokens_in.astype(jnp.float32)
    normed_one, scale_one = norm_apply(residual, gain_first, D, grid_total)
    wide_one = widen(normed_one.astype(jnp.bfloat16))
    mixer_in = spread(wide_one, kernel_in, False).astype(jnp.bfloat16)
    seq_count = mixer_in.shape[0] // SEQ_LEN
    by_sequence = mixer_in.reshape(seq_count, SEQ_LEN, mixer_in.shape[1])

    def front_seq(seq_in):
        return mixer_front(
            seq_in.astype(jnp.float32),
            conv_inner,
            conv_state,
            step_bias,
            decay_log,
            skip_scale,
            key_pick,
            HD,
        )

    gated, attended = lax.map(front_seq, by_sequence)
    gated = gated.reshape(-1, inner_local)
    attended = attended.reshape(-1, query_local)
    gated_norm, gated_scale = norm_apply(gated, mixer_gain, DI, head_total)
    mixed = jnp.concatenate([gated_norm, attended], axis=1).astype(jnp.bfloat16)
    mixed_long = lengthen(mixed)
    hidden = residual + narrow(plain_dot(mixed_long, kernel_out))
    normed_two, scale_two = norm_apply(hidden, gain_second, D, grid_total)
    wide_two = widen(normed_two.astype(jnp.bfloat16))
    gate_up = spread(wide_two, kernel_ffn, False)
    gate_val = gate_up[:, :ffn_local]
    up_val = gate_up[:, ffn_local:]
    active = (jax.nn.silu(gate_val) * up_val).astype(jnp.bfloat16)
    active_long = lengthen(active)
    block_out = (hidden + narrow(plain_dot(active_long, ffn_down))).astype(jnp.bfloat16)
    grad_out = out_grad.astype(jnp.float32)
    out_wide = widen(out_grad)
    d_active = spread(out_wide, ffn_down, True)
    grad_down = dot_tn(active_long, out_wide)
    sigmoid_gate = jax.nn.sigmoid(gate_val)
    d_gate = d_active * up_val * sigmoid_gate * (1.0 + gate_val * (1.0 - sigmoid_gate))
    d_up = d_active * gate_val * sigmoid_gate
    d_gate_up = jnp.concatenate([d_gate, d_up], axis=1).astype(jnp.bfloat16)
    d_gate_up_long = lengthen(d_gate_up)
    d_normed_two = narrow(dot_nt(d_gate_up_long, kernel_ffn))
    grad_gate_up = dot_tn(wide_two, d_gate_up_long)
    d_hidden_norm, grad_second = norm_back(
        hidden, scale_two, gain_second, d_normed_two, D, grid_total
    )
    d_hidden = grad_out + d_hidden_norm
    hidden_wide = widen(d_hidden.astype(jnp.bfloat16))
    d_mixed = spread(hidden_wide, kernel_out, True)
    grad_kernel_out = dot_tn(mixed_long, hidden_wide)
    d_gated, grad_gain_mix = norm_back(
        gated, gated_scale, mixer_gain, d_mixed[:, :inner_local], DI, head_total
    )
    d_attended = d_mixed[:, inner_local:]

    def local_front(values, kernel_one, kernel_two, bias_vec, decay_vec, skip_vec):
        return mixer_front(
            values, kernel_one, kernel_two, bias_vec, decay_vec, skip_vec, key_pick, HD
        )

    def back_seq(carry, items):
        seq_in, seq_gated, seq_attended = items
        _, pull = jax.vjp(
            local_front,
            seq_in.astype(jnp.float32),
            conv_inner,
            conv_state,
            step_bias,
            decay_log,
            skip_scale,
        )
        grads = pull((seq_gated, seq_attended))
        return (jax.tree.map(jnp.add, carry, tuple(grads[1:])), grads[0])

    start_grads = (
        jnp.zeros_like(conv_inner),
        jnp.zeros_like(conv_state),
        jnp.zeros_like(step_bias),
        jnp.zeros_like(decay_log),
        jnp.zeros_like(skip_scale),
    )
    mixer_grads, d_mixer_in = lax.scan(
        back_seq,
        start_grads,
        (
            by_sequence,
            d_gated.reshape(seq_count, SEQ_LEN, -1),
            d_attended.reshape(seq_count, SEQ_LEN, -1),
        ),
    )
    d_mixer_in = d_mixer_in.reshape(-1, d_mixer_in.shape[2]).astype(jnp.bfloat16)
    d_in_long = lengthen(d_mixer_in)
    d_normed_one = narrow(dot_nt(d_in_long, kernel_in))
    grad_kernel_in = dot_tn(wide_one, d_in_long)
    d_tokens_norm, grad_first = norm_back(
        residual, scale_one, gain_first, d_normed_one, D, grid_total
    )
    grad_tokens = (d_hidden + d_tokens_norm).astype(jnp.bfloat16)
    block_grad, ffn_grad, outer_grad, down_grad, first_sum, second_sum = lax.psum(
        (
            grad_kernel_in[:, :block_cols],
            grad_gate_up,
            grad_kernel_out,
            grad_down,
            grad_first,
            grad_second,
        ),
        "dp",
    )
    shared_grad = lax.psum(grad_kernel_in[:, block_cols:], ("dp", "col"))
    conv_sum, bias_sum, decay_sum, skip_sum, mixer_sum = lax.psum(
        (mixer_grads[0], mixer_grads[2], mixer_grads[3], mixer_grads[4], grad_gain_mix),
        ("dp", "row"),
    )
    state_sum = lax.psum(mixer_grads[1], ("dp", "row", "col"))
    first_col = 2 * inner_local
    return (
        block_out,
        grad_tokens,
        first_sum,
        block_grad[:, :inner_local],
        block_grad[:, inner_local:first_col],
        block_grad[:, first_col : first_col + step_local],
        block_grad[:, first_col + step_local :],
        shared_grad[:, :state_cols],
        shared_grad[:, state_cols:],
        conv_sum,
        state_sum,
        bias_sum,
        decay_sum,
        skip_sum,
        mixer_sum,
        outer_grad[:inner_local],
        outer_grad[inner_local:],
        second_sum,
        ffn_grad[:, :ffn_local],
        ffn_grad[:, ffn_local:],
        down_grad,
    )


def solution(mesh):
    in_specs = (
        P("dp", ("row", "col")),
        P(("row", "col")),
        P("row", "col"),
        P("row", "col"),
        P("row", "col"),
        P("row", "col"),
        P("row", None),
        P("row", None),
        P(None, "col"),
        P(),
        P("col"),
        P("col"),
        P("col"),
        P("col"),
        P("col", "row"),
        P("col", "row"),
        P(("row", "col")),
        P("row", "col"),
        P("row", "col"),
        P("col", "row"),
        P("dp", ("row", "col")),
    )
    out_specs = (
        P("dp", ("row", "col")),
        P("dp", ("row", "col")),
        P(("row", "col")),
        P("row", "col"),
        P("row", "col"),
        P("row", "col"),
        P("row", "col"),
        P("row", None),
        P("row", None),
        P(None, "col"),
        P(),
        P("col"),
        P("col"),
        P("col"),
        P("col"),
        P("col", "row"),
        P("col", "row"),
        P(("row", "col")),
        P("row", "col"),
        P("row", "col"),
        P("col", "row"),
    )
    return jax.shard_map(
        on_device, mesh=mesh, in_specs=in_specs, out_specs=out_specs, check_vma=False
    )
```

profile of v0, /device:TPU:0, one launch (start us, length us, event | category | flops | bytes accessed | tf_op | source)
XLA Modules:
  0.0 2293.5 jit_solution(798932154814564041)
XLA Ops:
  8.6 62.9 %psum.133 = f32[4096]{0:T(1024)S(1)} all-reduce(f32[4096]{0:T(1024)S(1)} %fusion.49), channel_id=1, replica_groups=mesh['dp'=2,'row'=4,'col'=4] {'row','col'}, use_global_device_ids=true, to_apply=%region_1.2 | all-reduce | flops 4096 | bytes 32768 | tf_op jit(solution)/shard_map/psum | solution.py:37
  74.9 19.3 all-gather.9.cloned.1.call-done
  94.2 12.5 fusion.126
  107.2 2.6 copy.71
  110.0 379.6 %reduce-scatter.9.cloned.1.call-done = f32[1024,1414]{0,1:T(8,128)} async-done(((f32[4096,1414]{0,1:T(8,128)}), f32[1024,1414]{0,1:T(8,128)}) %reduce-scatter.9.cloned.1.call-update) | async-done | bytes 5791760 | tf_op jit(solution)/shard_map/reduce_scatter | solution.py:63
  489.6 4.1 fusion.120
  496.8 2.1 fusion.59
  498.9 5.1 fusion.71
  506.3 2.7 fusion.40
  509.0 28.7 %bitcast_add_fusion = f32[1024,6,64]{0,2,1:T(8,128)S(1)} fusion(f32[1024,6,64]{0,2,1:T(8,128)S(1)} %bitcast.150, f32[1024,1024]{1,0:T(8,128)S(1)} %copy-done.25, f32[6,1024]{1,0:T(8,128)S(1)} %bitcast.164, pred[1024,1024]{1,0:T(8,128)(4,1)} %copy.71, f32[6]{0:T(128)S(1)} %copy-done.96, f32[1024,6]{0,1:T(8,128)S(1)} %get-tuple-element.218), kind=kOutput, calls=%fused_computation.79 | convolution fusion | flops 4858183680 | bytes 8437784 | tf_op jit(solution)/shard_map/while/body/eval_jaxpr/hts,shp->thp/dot_general | solution.py:122
  537.8 2.5 multiply_reduce_fusion.9
  540.3 6.9 psum.134
  547.2 2.4 gather_fusion.1
  551.0 5.9 fusion.19
  560.2 7.5 fusion.46
  569.2 81.7 %all-gather.11.cloned.1.call-done = bf16[4096,512]{0,1:T(8,128)(2,1)} async-done(((bf16[1024,512]{0,1:T(8,128)(2,1)}), bf16[4096,512]{0,1:T(8,128)(2,1)}) %all-gather.11.cloned.1.call-update) | async-done | bytes 4194320 | tf_op jit(solution)/shard_map/all_gather | solution.py:49
  650.8 5.5 fusion.127
  657.1 42.5 %reduce-scatter.11.cloned.1.call-done = f32[4096,64]{0,1:T(8,128)} async-done(((f32[4096,256]{0,1:T(8,128)}), f32[4096,64]{0,1:T(8,128)}) %reduce-scatter.11.cloned.1.call-update) | async-done | bytes 1048592 | tf_op jit(solution)/shard_map/reduce_scatter | solution.py:53
  701.0 60.9 %psum.135 = f32[4096]{0:T(1024)S(1)} all-reduce(f32[4096]{0:T(1024)S(1)} %get-tuple-element.213), channel_id=1, replica_groups=mesh['dp'=2,'row'=4,'col'=4] {'row','col'}, use_global_device_ids=true, to_apply=%region_11.13 | all-reduce | flops 4096 | bytes 32768 | tf_op jit(solution)/shard_map/psum | solution.py:37
  762.9 6.3 fusion.130
  771.2 11.6 all-gather.13.cloned.1.call-done
  782.8 10.3 fusion.128
  793.2 136.6 %reduce-scatter.17.cloned.1.call-done = f32[1024,512]{1,0:T(8,128)} async-done(((f32[4096,512]{1,0:T(8,128)}), f32[1024,512]{1,0:T(8,128)}) %reduce-scatter.17.cloned.1.call-update) | async-done | bytes 2097168 | tf_op jit(solution)/shard_map/reduce_scatter | solution.py:63
  929.8 283.5 %reduce-scatter.13.cloned.1.call-done = f32[1024,1024]{1,0:T(8,128)} async-done(((f32[4096,1024]{1,0:T(8,128)}), f32[1024,1024]{1,0:T(8,128)}) %reduce-scatter.13.cloned.1.call-update) | async-done | bytes 4194320 | tf_op jit(solution)/shard_map/reduce_scatter | solution.py:63
  1213.3 5.2 multiply_convert_fusion.1
  1220.2 150.5 %all-gather.19.cloned.1.call-done = bf16[4096,1024]{1,0:T(8,128)(2,1)} async-done(((bf16[1024,1024]{1,0:T(8,128)(2,1)}), bf16[4096,1024]{1,0:T(8,128)(2,1)}) %all-gather.19.cloned.1.call-update) | async-done | bytes 8388624 | tf_op jit(solution)/shard_map/all_gather | solution.py:49
  1370.7 7.8 fusion.131
  1378.5 42.8 %reduce-scatter.19.cloned.1.call-done = f32[4096,64]{0,1:T(8,128)} async-done(((f32[4096,256]{0,1:T(8,128)}), f32[4096,64]{0,1:T(8,128)}) %reduce-scatter.19.cloned.1.call-update) | async-done | bytes 1048592 | tf_op jit(solution)/shard_map/reduce_scatter | solution.py:53
  1421.4 2.1 multiply_reduce_fusion.10
  1423.5 60.2 %psum.136 = f32[4096]{0:T(1024)S(1)} all-reduce(f32[4096]{0:T(1024)S(1)} %get-tuple-element.180), channel_id=1, replica_groups=mesh['dp'=2,'row'=4,'col'=4] {'row','col'}, use_global_device_ids=true, to_apply=%region_17.19 | all-reduce | flops 4096 | bytes 32768 | tf_op jit(solution)/shard_map/psum | solution.py:37
  1484.3 2.3 fusion.111
  1486.7 19.9 all-gather.21.cloned.1.call-done
  1506.7 6.2 fusion.137
  1513.7 143.8 %reduce-scatter.21.cloned.1.call-done = f32[1024,512]{0,1:T(8,128)} async-done(((f32[4096,512]{0,1:T(8,128)}), f32[1024,512]{0,1:T(8,128)}) %reduce-scatter.21.cloned.1.call-update) | async-done | bytes 2097168 | tf_op jit(solution)/shard_map/reduce_scatter | solution.py:63
  1659.3 6.8 psum.137
  1666.2 5.5 multiply_reduce_fusion.3
  1671.7 34.6 %fusion.7 = (f32[6,1024]{1,0:T(8,128)S(1)}, f32[6,1024]{1,0:T(8,128)S(1)}, f32[1024,1024]{1,0:T(8,128)}) fusion(f32[1024,1024]{1,0:T(8,128)S(1)} %copy-done.26, f32[6,1024]{1,0:T(8,128)S(1)} %bitcast.165, pred[1024,1024]{1,0:T(8,128)(4,1)S(1)} %copy-done.46, f32[6,64,1024]{2,1,0:T(8,128)S(1)} %bitcast.153, f32[1024,6,64]{0,2,1:T(8,128)S(1)} %bitcast.152, ...), kind=kOutput, calls=%fused_computation.14 | convolution fusion | flops 4900376576 | bytes 12681216 | tf_op jit(solution)/shard_map/while/body/eval_jaxpr/transpose(jvp(hts,shp->thp))/dot_general | solution.py:122
  1706.4 7.4 reduce-window.16
  1715.3 12.8 fusion.30
  1728.2 13.6 multiply_reduce_fusion.1
  1742.7 8.1 convert_reduce_fusion
  1750.9 6.6 fusion.21
  1759.8 26.4 %fusion.37 = (f32[1024,6]{0,1:T(8,128)S(1)}, f32[1024,6,64]{0,2,1:T(8,128)}) fusion(f32[1024,6,64]{0,2,1:T(8,128)} %bitcast.151, f32[1024,6]{0,1:T(8,128)S(1)} %get-tuple-element.218, f32[1024,6,64]{0,2,1:T(8,128)} %bitcast.154, f32[6]{0:T(128)S(1)} %copy-done.96, f32[6,64,1024]{2,1,0:T(8,128)} %bitcast.155, f32[1024,1024]{1,0:T(8,128)} %fusion.71, ...), kind=kOutput, calls=%fused_computation.75 | convolution fusion | flops 4858963968 | bytes 11608088 | tf_op jit(solution)/shard_map/while/body/eval_jaxpr/transpose(jvp(hts,shp->thp))/dot_general | solution.py:122
  1787.2 5.6 fusion.69
  1792.8 2.7 fusion.73
  1795.5 2.4 multiply_reduce_fusion.14
  1801.0 3.3 multiply_reduce_fusion.7
  1807.7 8.1 fusion.20
  1815.8 2.1 add_convert_fusion
  1819.5 4.4 fusion.136
  1824.0 8.2 fusion.135
  1832.1 188.4 %all-gather.23.cloned.1.call-done = bf16[4096,1414]{0,1:T(8,128)(2,1)} async-done(((bf16[1024,1414]{0,1:T(8,128)(2,1)}), bf16[4096,1414]{0,1:T(8,128)(2,1)}) %all-gather.23.cloned.1.call-update) | async-done | bytes 11583504 | tf_op jit(solution)/shard_map/all_gather | solution.py:49
  2020.5 6.2 fusion.133
  2028.8 5.0 fusion.134
  2035.3 9.2 fusion.132
  2044.6 5.4 fusion.129
  2050.3 38.7 %psum.143 = f32[4,256]{1,0:T(4,128)} all-reduce(f32[4,256]{1,0:T(4,128)S(1)} %pad_add_fusion.6), channel_id=1, replica_groups=mesh['dp'=2,'row'=4,'col'=4] {'dp','row','col'}, use_global_device_ids=true, to_apply=%region_50.53 | all-reduce | flops 1024 | bytes 8192 | tf_op jit(solution)/shard_map/psum | solution.py:292
  2089.0 23.1 %all-reduce.26 = (f32[4,384]{1,0:T(4,128)}, f32[6]{0:T(128)}, f32[6]{0:T(128)}, f32[6]{0:T(128)}, f32[384]{0:T(512)}) all-reduce(f32[4,384]{1,0:T(4,128)S(1)} %pad_add_fusion.5, f32[6]{0:T(128)S(1)} %get-tuple-element.206, f32[6]{0:T(128)S(1)} %negate_multiply_fusion, ...), channel_id=1, replica_groups=mesh['dp'=2,'row'=4,'col'=4] {'dp','row'}, use_global_device_ids=true, to_apply=%region_45.48 | all-reduce | flops 1938 | bytes 15504 | tf_op jit(solution)/shard_map/psum | solution.py:288
  2114.8 53.5 %all-reduce.34.cloned.1.call-done = (f32[256,902]{0,1:T(8,128)}, f32[512,256]{1,0:T(8,128)}, f32[256,1024]{1,0:T(8,128)}, f32[512,256]{1,0:T(8,128)}) async-done(((f32[256,902]{0,1:T(8,128)}, f32[512,256]{1,0:T(8,128)}, f32[256,1024]{1,0:T(8,128)}, f32[512,256]{1,0:T(8,128)}), (f32[256,902]{0,1:T(8,128)}, f32[512,256]{1,0:T(8,128)}, f32[256,1024]{1,0:T(8,128)}, ...) | async-done | bytes 3020816 | tf_op jit(solution)/shard_map/psum | solution.py:276
  2177.7 2.6 fusion.122
  2180.3 35.3 %reduce-scatter.23.cloned.1.call-done = f32[4096,64]{0,1:T(8,128)} async-done(((f32[4096,256]{0,1:T(8,128)}), f32[4096,64]{0,1:T(8,128)}) %reduce-scatter.23.cloned.1.call-update) | async-done | bytes 1048592 | tf_op jit(solution)/shard_map/reduce_scatter | solution.py:53
  2217.2 5.4 all-reduce.27
  2222.7 59.8 %psum.138 = f32[4096]{0:T(1024)S(1)} all-reduce(f32[4096]{0:T(1024)S(1)} %get-tuple-element.186), channel_id=1, replica_groups=mesh['dp'=2,'row'=4,'col'=4] {'row','col'}, use_global_device_ids=true, to_apply=%region_36.39 | all-reduce | flops 4096 | bytes 32768 | tf_op jit(solution)/shard_map/psum | solution.py:37
  2282.6 3.1 fusion.55
  (327 shorter events, 58.6 us)
Async XLA Ops:
  7.2 755.7 %copy-start = (bf16[512,256]{1,0:T(8,128)(2,1)S(1)}, bf16[512,256]{1,0:T(8,128)(2,1)}, u32[]{:S(2)}) copy-start(bf16[512,256]{1,0:T(8,128)(2,1)} %param.44) | copy-start | bytes 786436
  7.2 67.0 %copy-start.89 = (bf16[256,6]{0,1:T(8,128)(2,1)S(1)}, bf16[256,6]{0,1:T(8,128)(2,1)}, u32[]{:S(2)}) copy-start(bf16[256,6]{0,1:T(8,128)(2,1)} %param.29) | copy-start | bytes 9220
  7.2 67.2 %copy-start.53 = (bf16[256,384]{1,0:T(8,128)(2,1)S(1)}, bf16[256,384]{1,0:T(8,128)(2,1)}, u32[]{:S(2)}) copy-start(bf16[256,384]{1,0:T(8,128)(2,1)} %param.27) | copy-start | bytes 589828
  7.2 67.2 %copy-start.54 = (bf16[256,384]{1,0:T(8,128)(2,1)S(1)}, bf16[256,384]{1,0:T(8,128)(2,1)}, u32[]{:S(2)}) copy-start(bf16[256,384]{1,0:T(8,128)(2,1)} %param.28) | copy-start | bytes 589828
  7.2 67.2 %copy-start.62 = (bf16[256,128]{1,0:T(8,128)(2,1)S(1)}, bf16[256,128]{1,0:T(8,128)(2,1)}, u32[]{:S(2)}) copy-start(bf16[256,128]{1,0:T(8,128)(2,1)} %param.30) | copy-start | bytes 196612
  7.2 67.2 %copy-start.60 = (bf16[256,256]{1,0:T(8,128)(2,1)S(1)}, bf16[256,256]{1,0:T(8,128)(2,1)}, u32[]{:S(2)}) copy-start(bf16[256,256]{1,0:T(8,128)(2,1)} %param.31) | copy-start | bytes 393220
  7.3 67.2 %copy-start.61 = (bf16[256,256]{1,0:T(8,128)(2,1)S(1)}, bf16[256,256]{1,0:T(8,128)(2,1)}, u32[]{:S(2)}) copy-start(bf16[256,256]{1,0:T(8,128)(2,1)} %param.32) | copy-start | bytes 393220
  7.3 87.0 %all-gather.9.cloned.1.call-start = ((), (), s32[]{:S(2)}) async-start(), calls=%async_computation.8 | async-start | bytes 2621440 | tf_op jit(solution)/shard_map/all_gather | solution.py:45
  74.2 415.4 %reduce-scatter.9.cloned.1.call-start = ((), (), s32[]{:S(2)}) async-start(), calls=%async_computation.9 | async-start | bytes 28999680 | tf_op jit(solution)/shard_map/reduce_scatter | solution.py:63
  74.9 31.8 %copy-start.31 = (bf16[256,1414]{1,0:T(8,128)(2,1)}, bf16[256,1414]{1,0:T(8,128)(2,1)S(1)}, u32[]{:S(2)}) copy-start(bf16[256,1414]{1,0:T(8,128)(2,1)S(1)} %concatenate.29) | copy-start | bytes 2171908
  106.8 544.1 %all-gather.11.cloned.1.call-start = ((), (), s32[]{:S(2)}) async-start(), calls=%async_computation.10 | async-start | bytes 5242880 | tf_op jit(solution)/shard_map/all_gather | solution.py:49
  107.1 451.7 %copy-start.6 = (pred[1024,1024]{0,1:T(8,128)(4,1)}, pred[1024,1024]{0,1:T(8,128)(4,1)S(1)}, u32[]{:S(2)}) copy-start(pred[1024,1024]{0,1:T(8,128)(4,1)S(1)} %iota_compare_fusion) | copy-start | bytes 3145732
  109.7 384.0 %copy-start.86 = (s32[2]{0:T(128)}, s32[2]{0:T(128)S(1)}, u32[]{:S(2)}) copy-start(s32[2]{0:T(128)S(1)} %compare_select_fusion.3) | copy-start | bytes 28
  109.8 396.4 %copy-start.66 = (f32[384]{0:T(512)}, f32[384]{0:T(512)S(1)}, u32[]{:S(2)}) copy-start(f32[384]{0:T(512)S(1)} %get-tuple-element.189) | copy-start | bytes 4612
  109.8 396.4 %copy-start.68 = (f32[384]{0:T(512)}, f32[384]{0:T(512)S(1)}, u32[]{:S(2)}) copy-start(f32[384]{0:T(512)S(1)} %get-tuple-element.190) | copy-start | bytes 4612
  109.9 396.4 %copy-start.70 = (f32[384]{0:T(512)}, f32[384]{0:T(512)S(1)}, u32[]{:S(2)}) copy-start(f32[384]{0:T(512)S(1)} %get-tuple-element.191) | copy-start | bytes 4612
  109.9 396.4 %copy-start.72 = (f32[384]{0:T(512)}, f32[384]{0:T(512)S(1)}, u32[]{:S(2)}) copy-start(f32[384]{0:T(512)S(1)} %get-tuple-element.188) | copy-start | bytes 4612
  109.9 394.1 %copy-start.93 = (f32[6]{0:T(128)}, f32[6]{0:T(128)S(1)}, u32[]{:S(2)}) copy-start(f32[6]{0:T(128)S(1)} %exponential_negate_fusion) | copy-start | bytes 76
  109.9 386.8 %copy-start.75 = (f32[1,256]{1,0:T(1,128)}, f32[1,256]{1,0:T(1,128)S(1)}, u32[]{:S(2)}) copy-start(f32[1,256]{1,0:T(1,128)S(1)} %get-tuple-element.251) | copy-start | bytes 3076
  109.9 386.8 %copy-start.77 = (f32[1,256]{1,0:T(1,128)}, f32[1,256]{1,0:T(1,128)S(1)}, u32[]{:S(2)}) copy-start(f32[1,256]{1,0:T(1,128)S(1)} %get-tuple-element.252) | copy-start | bytes 3076
  110.0 386.8 %copy-start.79 = (f32[1,256]{1,0:T(1,128)}, f32[1,256]{1,0:T(1,128)S(1)}, u32[]{:S(2)}) copy-start(f32[1,256]{1,0:T(1,128)S(1)} %get-tuple-element.253) | copy-start | bytes 3076
  110.0 386.8 %copy-start.81 = (f32[1,256]{1,0:T(1,128)}, f32[1,256]{1,0:T(1,128)S(1)}, u32[]{:S(2)}) copy-start(f32[1,256]{1,0:T(1,128)S(1)} %get-tuple-element.250) | copy-start | bytes 3076
  509.0 28.7 %copy-start.40 = (f32[1024,384]{0,1:T(8,128)}, f32[1024,384]{0,1:T(8,128)S(1)}, u32[]{:S(2)}) copy-start(f32[1024,384]{0,1:T(8,128)S(1)} %get-tuple-element.223) | copy-start | bytes 4718596
  569.0 130.5 %reduce-scatter.11.cloned.1.call-start = ((), (), s32[]{:S(2)}) async-start(), calls=%async_computation.11 | async-start | bytes 5242880 | tf_op jit(solution)/shard_map/reduce_scatter | solution.py:53
  569.1 87.2 %copy-start.39 = (bf16[512,256]{1,0:T(8,128)(2,1)}, bf16[512,256]{1,0:T(8,128)(2,1)S(1)}, u32[]{:S(2)}) copy-start(bf16[512,256]{1,0:T(8,128)(2,1)S(1)} %constant_dynamic-update-slice_fusion) | copy-start | bytes 786436
  656.4 43.2 %copy-start.13 = (bf16[4096,64]{0,1:T(8,128)(2,1)S(1)}, bf16[4096,64]{0,1:T(8,128)(2,1)}, u32[]{:S(2)}) copy-start(bf16[4096,64]{0,1:T(8,128)(2,1)} %param.25) | copy-start | bytes 1572868
  656.4 105.5 %copy-start.83 = (f32[64]{0:T(128)S(1)}, f32[64]{0:T(128)}, u32[]{:S(2)}) copy-start(f32[64]{0:T(128)} %param.41) | copy-start | bytes 772
  656.4 106.5 %all-gather.17.cloned.1.call-start = ((), (), s32[]{:S(2)}) async-start(), calls=%async_computation.16 | async-start | bytes 2621440 | tf_op jit(solution)/shard_map/all_gather | solution.py:45
  657.0 125.8 %all-gather.13.cloned.1.call-start = ((), (), s32[]{:S(2)}) async-start(), calls=%async_computation.12 | async-start | bytes 2621440 | tf_op jit(solution)/shard_map/all_gather | solution.py:45
  701.0 782.7 %copy-start.2 = (f32[4096,64]{0,1:T(8,128)}, f32[4096,64]{0,1:T(8,128)S(1)}, u32[]{:S(2)}) copy-start(f32[4096,64]{0,1:T(8,128)S(1)} %get-tuple-element.214) | copy-start | bytes 3145732
  761.9 721.9 %copy-start.48 = (f32[4096]{0:T(1024)}, f32[4096]{0:T(1024)S(1)}, u32[]{:S(2)}) copy-start(f32[4096]{0:T(1024)S(1)} %add_rsqrt_fusion) | copy-start | bytes 49156
  762.8 167.0 %reduce-scatter.17.cloned.1.call-start = ((), (), s32[]{:S(2)}) async-start(), calls=%async_computation.17 | async-start | bytes 10485760 | tf_op jit(solution)/shard_map/reduce_scatter | solution.py:63
  769.2 444.1 %reduce-scatter.13.cloned.1.call-start = ((), (), s32[]{:S(2)}) async-start(), calls=%async_computation.13 | async-start | bytes 20971520 | tf_op jit(solution)/shard_map/reduce_scatter | solution.py:63
  793.2 577.5 %all-gather.19.cloned.1.call-start = ((), (), s32[]{:S(2)}) async-start(), calls=%async_computation.18 | async-start | bytes 10485760 | tf_op jit(solution)/shard_map/all_gather | solution.py:49
  1220.1 201.2 %reduce-scatter.19.cloned.1.call-start = ((), (), s32[]{:S(2)}) async-start(), calls=%async_computation.19 | async-start | bytes 5242880 | tf_op jit(solution)/shard_map/reduce_scatter | solution.py:53
  1378.5 105.9 %copy-start.23 = (bf16[4096,64]{0,1:T(8,128)(2,1)S(1)}, bf16[4096,64]{0,1:T(8,128)(2,1)}, u32[]{:S(2)}) copy-start(bf16[4096,64]{0,1:T(8,128)(2,1)} %param.45) | copy-start | bytes 1572868
  1378.5 128.2 %all-gather.21.cloned.1.call-start = ((), (), s32[]{:S(2)}) async-start(), calls=%async_computation.20 | async-start | bytes 2621440 | tf_op jit(solution)/shard_map/all_gather | solution.py:45
  1486.7 170.8 %reduce-scatter.21.cloned.1.call-start = ((), (), s32[]{:S(2)}) async-start(), calls=%async_computation.21 | async-start | bytes 10485760 | tf_op jit(solution)/shard_map/reduce_scatter | solution.py:63
  1512.8 305.2 %all-gather.15.cloned.1.call-start = ((), (), s32[]{:S(2)}) async-start(), calls=%async_computation.14 | async-start | bytes 5242880 | tf_op jit(solution)/shard_map/all_gather | solution.py:49
  1512.9 153.2 %copy-start.11 = (f32[1024,384]{0,1:T(8,128)S(1)}, f32[1024,384]{0,1:T(8,128)}, u32[]{:S(2)}) copy-start(f32[1024,384]{0,1:T(8,128)} %get-tuple-element.224) | copy-start | bytes 4718596
  1513.6 506.9 %all-gather.23.cloned.1.call-start = ((), (), s32[]{:S(2)}) async-start(), calls=%async_computation.22 | async-start | bytes 14499840 | tf_op jit(solution)/shard_map/all_gather | solution.py:49
  1671.7 34.7 %copy-start.43 = (f32[1024,384]{0,1:T(8,128)}, f32[1024,384]{0,1:T(8,128)S(1)}, u32[]{:S(2)}) copy-start(f32[1024,384]{0,1:T(8,128)S(1)} %get-tuple-element.205) | copy-start | bytes 4718596
  1671.7 43.6 %copy-start.7 = (pred[1024,1024]{0,1:T(8,128)(4,1)S(1)}, pred[1024,1024]{0,1:T(8,128)(4,1)}, u32[]{:S(2)}) copy-start(pred[1024,1024]{0,1:T(8,128)(4,1)} %copy-done.6) | copy-start | bytes 3145732
  1728.2 13.6 copy-start.87
  1759.8 26.4 %copy-start.92 = (f32[6]{0:T(128)S(1)}, f32[6]{0:T(128)}, u32[]{:S(2)}) copy-start(f32[6]{0:T(128)} %param.35) | copy-start | bytes 76
  1759.8 26.4 %copy-start.94 = (f32[6]{0:T(128)S(1)}, f32[6]{0:T(128)}, u32[]{:S(2)}) copy-start(f32[6]{0:T(128)} %copy-done.93) | copy-start | bytes 76
  1759.8 27.4 %copy-start.5 = (f32[1024,1024]{1,0:T(8,128)S(1)}, f32[1024,1024]{1,0:T(8,128)}, u32[]{:S(2)}) copy-start(f32[1024,1024]{1,0:T(8,128)} %get-tuple-element.173) | copy-start | bytes 12582916
  1818.0 294.1 %all-reduce.32.cloned.1.call-start = ((), (), s32[]{:S(2)}) async-start(), calls=%async_computation.24 | async-start | bytes 1048576 | tf_op jit(solution)/shard_map/psum | solution.py:287
  1824.0 196.6 %copy-start.29 = (bf16[4096,256]{0,1:T(8,128)(2,1)S(1)}, bf16[4096,256]{0,1:T(8,128)(2,1)}, u32[]{:S(2)}) copy-start(bf16[4096,256]{0,1:T(8,128)(2,1)} %all-gather.9.cloned.1.call-done) | copy-start | bytes 6291460
  2028.8 139.5 %all-reduce.34.cloned.1.call-start = ((), (), s32[]{:S(2)}) async-start(), calls=%async_computation.25 | async-start | bytes 6045696 | tf_op jit(solution)/shard_map/psum | solution.py:276
  2034.9 180.7 %reduce-scatter.23.cloned.1.call-start = ((), (), s32[]{:S(2)}) async-start(), calls=%async_computation.23 | async-start | bytes 5242880 | tf_op jit(solution)/shard_map/reduce_scatter | solution.py:53
  2044.6 237.9 %reduce-scatter.15.cloned.1.call-start = ((), (), s32[]{:S(2)}) async-start(), calls=%async_computation.15 | async-start | bytes 5242880 | tf_op jit(solution)/shard_map/reduce_scatter | solution.py:53
  2050.1 39.0 %copy-start.98 = (f32[6]{0:T(128)S(1)}, f32[6]{0:T(128)}, u32[]{:S(2)}) copy-start(f32[6]{0:T(128)} %param.36) | copy-start | bytes 76
  2175.0 40.6 %copy-start.14 = (bf16[4096,64]{0,1:T(8,128)(2,1)S(1)}, bf16[4096,64]{0,1:T(8,128)(2,1)}, u32[]{:S(2)}) copy-start(bf16[4096,64]{0,1:T(8,128)(2,1)} %param.25) | copy-start | bytes 1572868
  2176.9 105.7 %copy-start.3 = (f32[4096,64]{0,1:T(8,128)S(1)}, f32[4096,64]{0,1:T(8,128)}, u32[]{:S(2)}) copy-start(f32[4096,64]{0,1:T(8,128)} %copy-done.2) | copy-start | bytes 3145732
  2176.9 105.7 %copy-start.17 = (f32[4096,64]{0,1:T(8,128)S(1)}, f32[4096,64]{0,1:T(8,128)}, u32[]{:S(2)}) copy-start(f32[4096,64]{0,1:T(8,128)} %reduce-scatter.19.cloned.1.call-done) | copy-start | bytes 3145732
  2176.9 105.7 %copy-start.24 = (bf16[4096,64]{0,1:T(8,128)(2,1)S(1)}, bf16[4096,64]{0,1:T(8,128)(2,1)}, u32[]{:S(2)}) copy-start(bf16[4096,64]{0,1:T(8,128)(2,1)} %param.45) | copy-start | bytes 1572868
  2176.9 105.7 %copy-start.49 = (f32[4096]{0:T(1024)S(1)}, f32[4096]{0:T(1024)}, u32[]{:S(2)}) copy-start(f32[4096]{0:T(1024)} %copy-done.48) | copy-start | bytes 49156
  2177.6 39.6 %copy-start.95 = (f32[64]{0:T(128)S(1)}, f32[64]{0:T(128)}, u32[]{:S(2)}) copy-start(f32[64]{0:T(128)} %get-tuple-element.179) | copy-start | bytes 772
  2177.6 104.8 %copy-start.59 = (f32[4096]{0:T(1024)S(1)}, f32[4096]{0:T(1024)}, u32[]{:S(2)}) copy-start(f32[4096]{0:T(1024)} %copy-done.58) | copy-start | bytes 49156
  2177.6 104.9 %copy-start.51 = (f32[4096]{0:T(1024)S(1)}, f32[4096]{0:T(1024)}, u32[]{:S(2)}) copy-start(f32[4096]{0:T(1024)} %copy-done.50) | copy-start | bytes 49156
  2177.6 104.9 %copy-start.57 = (f32[4096]{0:T(1024)S(1)}, f32[4096]{0:T(1024)}, u32[]{:S(2)}) copy-start(f32[4096]{0:T(1024)} %copy-done.56) | copy-start | bytes 49156
  2177.6 104.9 %copy-start.84 = (f32[64]{0:T(128)S(1)}, f32[64]{0:T(128)}, u32[]{:S(2)}) copy-start(f32[64]{0:T(128)} %param.41) | copy-start | bytes 772
  2177.7 104.9 %copy-start.88 = (f32[64]{0:T(128)S(1)}, f32[64]{0:T(128)}, u32[]{:S(2)}) copy-start(f32[64]{0:T(128)} %param.26) | copy-start | bytes 772
  (55 other events, 215.6 us)
Sparse Core Ops, SparseCore 0:
  74.3 19.8 all-gather.8
  106.9 382.7 reduce-scatter.8
  569.2 81.6 all-gather.10
  656.5 43.0 reduce-scatter.10
  701.1 22.9 all-gather.16
  763.0 19.8 all-gather.12
  785.3 144.4 reduce-scatter.16
  932.3 281.0 reduce-scatter.12
  1220.3 150.3 all-gather.18
  1378.6 42.7 reduce-scatter.18
  1486.8 19.8 all-gather.20
  1513.0 144.4 reduce-scatter.20
  1659.1 81.4 all-gather.14
  1818.1 202.3 all-gather.22
  2028.9 52.7 all-reduce.31
  2084.5 83.7 all-reduce.33
  2170.8 44.7 reduce-scatter.22
  2218.0 45.0 reduce-scatter.14
where the time goes:
time: 2300 us; the launch traced here: 2290 us
  waiting for transfers between devices  1590 us (69%)
  blocking collectives  325 us (14%)
  matrix products  245 us (11%)
  other arithmetic  76.7 us (3%)
  local copies, waits for them, and re-layouts  40.2 us (2%)
    reduce_scatter x4, waiting for transfers between devices, spread(): return lax.psum_scatter(term(), 'row', scatter_dimension=0, tiled=True)  944 us
    all_gather x4, waiting for transfers between devices, lengthen(): return lax.all_gather(values, 'row', axis=0, tiled=True)  421 us
    psum x4, blocking collectives, grid_total(): return lax.psum(values, ('row', 'col'))  244 us
    reduce_scatter x4, waiting for transfers between devices, narrow(): return lax.psum_scatter(partial_sum, 'col', scatter_dimension=1, tiled=True)  121 us
    dot_general x3, matrix products, mixer_front(): jnp.einsum('hts,shp->thp', mixing * affinity[None], scaled_inner, precisi...  89.7 us
    psum x1, waiting for transfers between devices, on_device(): lax.psum((grad_kernel_in[:, :block_cols], grad_gate_up, grad_kernel_out,...  53.5 us
    all_gather x4, waiting for transfers between devices, widen(): return lax.all_gather(values, 'col', axis=1, tiled=True)  50.9 us
  transfers between devices with their start and end apart: 18, of which 14 were waited for; matrix products, arithmetic and copies ran while one was open for 10% of the time, Pallas kernels for 0%

commit v1 on v0

v1 whole, which is shorter than its diff:
```python
import math

import jax
import jax.numpy as jnp
from jax import lax
from jax.sharding import PartitionSpec as P

D = 1024
HQ = 8
HK = 2
HD = 64
DI = 1536
SEQ_LEN = 1024
CHUNK = 128


EPS = 1e-06
HIGH = lax.Precision.HIGHEST


def plain_dot(left, right):
    return jnp.dot(left, right, preferred_element_type=jnp.float32)


def dot_nt(left, right):
    return lax.dot_general(
        left, right, (((1,), (1,)), ((), ())), preferred_element_type=jnp.float32
    )


def dot_tn(left, right):
    return lax.dot_general(
        left, right, (((0,), (0,)), ((), ())), preferred_element_type=jnp.float32
    )


def gather_rows(weight):
    return lax.all_gather(weight, "row", axis=0, tiled=True)


def gather_tokens(values):
    return lax.all_gather(values, "col", axis=0, tiled=True)


def sum_tokens(partial_sum):
    return lax.psum_scatter(
        partial_sum.astype(jnp.bfloat16), "col", scatter_dimension=0, tiled=True
    ).astype(jnp.float32)


def sum_weight(partial_sum):
    return lax.psum_scatter(
        partial_sum.astype(jnp.bfloat16), "row", scatter_dimension=0, tiled=True
    )


def norm_apply(values, gain_vec):
    row_scale = lax.rsqrt(jnp.mean(values * values, axis=1) + EPS)
    return (values * row_scale[:, None] * gain_vec, row_scale)


def norm_back(values, row_scale, gain_vec, grads, width_all, total_fn):
    inner = total_fn(jnp.sum(grads * gain_vec * values, axis=1))
    d_values = (
        grads * gain_vec * row_scale[:, None] - values * (inner * row_scale**3 / width_all)[:, None]
    )
    d_gain = jnp.sum(grads * values * row_scale[:, None], axis=0)
    return (d_values, d_gain)


def causal_conv(signal, kernel):
    tap_count = kernel.shape[0]
    length = signal.shape[0]
    padded = jnp.concatenate(
        [jnp.zeros((tap_count - 1, signal.shape[1]), jnp.float32), signal], axis=0
    )
    result = kernel[tap_count - 1] * signal
    for offset in range(tap_count - 1):
        result = result + kernel[offset] * padded[offset : offset + length]
    return result


def per_channel(values, head_width):
    wide = jnp.broadcast_to(values[..., None], values.shape + (head_width,))
    return wide.reshape(values.shape[:-1] + (values.shape[-1] * head_width,))


def batch_dot(spec, left, right):
    return jnp.einsum(
        spec,
        left.astype(jnp.bfloat16),
        right.astype(jnp.bfloat16),
        preferred_element_type=jnp.float32,
    )


def state_space(step_decay, scaled_inner, b_matrix, c_matrix):
    length, heads = step_decay.shape
    width = scaled_inner.shape[1]
    head_width = width // heads
    chunks = length // CHUNK
    order = jnp.arange(CHUNK)
    causal = order[:, None] >= order[None, :]
    decay = jnp.einsum(
        "ts,csh->cth",
        causal.astype(jnp.float32),
        step_decay.reshape(chunks, CHUNK, heads),
        precision=HIGH,
    )
    whole = decay[:, -1]
    by_head = decay.transpose(0, 2, 1)
    spans = by_head[:, :, :, None] - by_head[:, :, None, :]
    mixing = jnp.where(causal, jnp.exp(jnp.where(causal, spans, 0.0)), 0.0)
    b_chunks = b_matrix.reshape(chunks, CHUNK, -1)
    c_chunks = c_matrix.reshape(chunks, CHUNK, -1)
    inner = scaled_inner.reshape(chunks, CHUNK, width)
    affinity = batch_dot("ctn,csn->cts", c_chunks, b_chunks)
    within = batch_dot(
        "chts,cshp->cthp",
        mixing * affinity[:, None],
        inner.reshape(chunks, CHUNK, heads, head_width),
    ).reshape(chunks, CHUNK, width)
    to_end = per_channel(jnp.exp(whole[:, None] - decay), head_width)
    added = batch_dot("csn,csq->cnq", b_chunks, inner * to_end)
    kept = per_channel(jnp.exp(whole), head_width)
    state = jnp.zeros_like(added[0])
    states = []
    for index in range(chunks):
        states.append(state)
        state = state * kept[index] + added[index]
    across = batch_dot("ctn,cnq->ctq", c_chunks, jnp.stack(states))
    across = across * per_channel(jnp.exp(decay), head_width)
    return (within + across).reshape(length, width)


def mixer_front(
    inputs, conv_inner, conv_state, step_bias, decay_log, skip_scale, key_pick, head_dim
):
    inner_width = conv_inner.shape[1]
    mamba_heads = step_bias.shape[0]
    head_width = inner_width // mamba_heads
    state_size = conv_state.shape[1] // 2
    query_width = key_pick.shape[0] * head_dim
    length = inputs.shape[0]
    gate_part = inputs[:, :inner_width]
    inner_part = inputs[:, inner_width : 2 * inner_width]
    first_col = 2 * inner_width
    step_part = inputs[:, first_col : first_col + mamba_heads]
    first_col = first_col + mamba_heads
    query_part = inputs[:, first_col : first_col + query_width]
    first_col = first_col + query_width
    state_part = inputs[:, first_col : first_col + 2 * state_size]
    keyval_part = inputs[:, first_col + 2 * state_size :]
    positions = jnp.arange(length)
    causal = positions[:, None] >= positions[None, :]
    mixed_inner = jax.nn.silu(causal_conv(inner_part, conv_inner))
    mixed_state = jax.nn.silu(causal_conv(state_part, conv_state))
    b_matrix = mixed_state[:, :state_size]
    c_matrix = mixed_state[:, state_size:]
    step_size = jax.nn.softplus(step_part + step_bias)
    ssm_out = state_space(
        step_size * -jnp.exp(decay_log),
        mixed_inner * per_channel(step_size, head_width),
        b_matrix,
        c_matrix,
    )
    ssm_out = ssm_out + per_channel(skip_scale, head_width) * mixed_inner
    gated = ssm_out * jax.nn.silu(gate_part)
    key_heads = keyval_part.shape[1] // (2 * head_dim)
    queries = query_part.reshape(length, -1, head_dim)
    keys_all = keyval_part[:, : key_heads * head_dim].reshape(length, key_heads, head_dim)
    values_all = keyval_part[:, key_heads * head_dim :].reshape(length, key_heads, head_dim)
    picked = (key_pick[:, None] == jnp.arange(key_heads)[None, :]).astype(jnp.float32)
    keys_used = batch_dot("hk,skd->shd", picked, keys_all)
    values_used = batch_dot("hk,skd->shd", picked, values_all)
    scores = batch_dot("thd,shd->hts", queries, keys_used) / math.sqrt(head_dim)
    scores = jnp.where(causal[None], scores, -1e30)
    peak = lax.stop_gradient(jnp.max(scores, axis=2, keepdims=True))
    weights = jnp.exp(scores - peak)
    weights = weights / jnp.sum(weights, axis=2, keepdims=True)
    attended = batch_dot("hts,shd->thd", weights, values_used).reshape(length, -1)
    return (gated, attended)


def on_device(
    tokens_in,
    gain_first,
    proj_gate,
    proj_inner,
    proj_step,
    proj_query,
    proj_state,
    proj_keyval,
    conv_inner,
    conv_state,
    step_bias,
    decay_log,
    skip_scale,
    mixer_gain,
    out_mamba,
    out_attn,
    gain_second,
    ffn_gate,
    ffn_up,
    ffn_down,
    out_grad,
):
    inner_local = proj_gate.shape[1]
    step_local = proj_step.shape[1]
    query_local = proj_query.shape[1]
    block_cols = 2 * inner_local + step_local + query_local
    state_cols = proj_state.shape[1]
    ffn_local = ffn_gate.shape[1]
    gain_local = gain_first.shape[0]
    heads_local = query_local // HD
    key_pick = (lax.axis_index("col") * heads_local + jnp.arange(heads_local)) // (HQ // HK)

    entering = lax.all_to_all(
        jnp.stack([tokens_in, out_grad]),
        ("row", "col"),
        split_axis=1,
        concat_axis=2,
        tiled=True,
    )
    gains = lax.all_gather(
        jnp.stack([gain_first, gain_second]), ("row", "col"), axis=1, tiled=True
    )
    kernel_in = gather_rows(
        jnp.concatenate(
            [proj_gate, proj_inner, proj_step, proj_query, proj_state, proj_keyval], axis=1
        )
    )
    kernel_out = gather_rows(jnp.concatenate([out_mamba, out_attn], axis=0).T)
    kernel_ffn = gather_rows(jnp.concatenate([ffn_gate, ffn_up, ffn_down.T], axis=1))
    kernel_gate_up = kernel_ffn[:, : 2 * ffn_local]
    kernel_down = kernel_ffn[:, 2 * ffn_local :]

    residual = entering[0].astype(jnp.float32)
    normed_one, scale_one = norm_apply(residual, gains[0])
    wide_one = gather_tokens(normed_one.astype(jnp.bfloat16))
    mixer_in = plain_dot(wide_one, kernel_in).astype(jnp.bfloat16)
    seq_count = mixer_in.shape[0] // SEQ_LEN

    def local_front(values, kernel_one, kernel_two, bias_vec, decay_vec, skip_vec):
        parts = [
            mixer_front(
                values[index * SEQ_LEN : (index + 1) * SEQ_LEN],
                kernel_one,
                kernel_two,
                bias_vec,
                decay_vec,
                skip_vec,
                key_pick,
                HD,
            )
            for index in range(seq_count)
        ]
        return tuple(jnp.concatenate(side, axis=0) for side in zip(*parts))

    (gated, attended), pull = jax.vjp(
        local_front,
        mixer_in.astype(jnp.float32),
        conv_inner,
        conv_state,
        step_bias,
        decay_log,
        skip_scale,
    )
    gated_scale = lax.rsqrt(lax.psum(jnp.sum(gated * gated, axis=1), "col") / DI + EPS)
    gated_norm = gated * gated_scale[:, None] * mixer_gain
    mixed = jnp.concatenate([gated_norm, attended], axis=1).astype(jnp.bfloat16)
    hidden = residual + sum_tokens(dot_nt(mixed, kernel_out))
    normed_two, scale_two = norm_apply(hidden, gains[1])
    wide_two = gather_tokens(normed_two.astype(jnp.bfloat16))
    out_wide = gather_tokens(entering[1])
    gate_up = plain_dot(wide_two, kernel_gate_up)
    gate_val = gate_up[:, :ffn_local]
    up_val = gate_up[:, ffn_local:]
    sigmoid_gate = jax.nn.sigmoid(gate_val)
    active = (gate_val * sigmoid_gate * up_val).astype(jnp.bfloat16)
    d_active = plain_dot(out_wide, kernel_down)
    d_gate = d_active * up_val * sigmoid_gate * (1.0 + gate_val * (1.0 - sigmoid_gate))
    d_up = d_active * gate_val * sigmoid_gate
    d_gate_up = jnp.concatenate([d_gate, d_up], axis=1).astype(jnp.bfloat16)
    d_normed_two = sum_tokens(dot_nt(d_gate_up, kernel_gate_up))
    ffn_part = sum_weight(
        jnp.concatenate([dot_tn(wide_two, d_gate_up), dot_tn(out_wide, active)], axis=1)
    )
    block_out = (hidden + sum_tokens(dot_nt(active, kernel_down))).astype(jnp.bfloat16)

    def whole_row(values):
        return values

    d_hidden_norm, grad_second = norm_back(
        hidden, scale_two, gains[1], d_normed_two, D, whole_row
    )
    d_hidden = entering[1].astype(jnp.float32) + d_hidden_norm
    hidden_wide = gather_tokens(d_hidden.astype(jnp.bfloat16))
    d_mixed = plain_dot(hidden_wide, kernel_out)
    d_gated, grad_gain_mix = norm_back(
        gated,
        gated_scale,
        mixer_gain,
        d_mixed[:, :inner_local],
        DI,
        lambda values: lax.psum(values, "col"),
    )
    mixer_grads = pull((d_gated, d_mixed[:, inner_local:]))
    d_mixer_in = mixer_grads[0].astype(jnp.bfloat16)
    d_normed_one = sum_tokens(dot_nt(d_mixer_in, kernel_in))
    d_tokens_norm, grad_first = norm_back(
        residual, scale_one, gains[0], d_normed_one, D, whole_row
    )
    grad_tokens = (d_hidden + d_tokens_norm).astype(jnp.bfloat16)
    leaving = lax.all_to_all(
        jnp.stack([block_out, grad_tokens]),
        ("row", "col"),
        split_axis=2,
        concat_axis=1,
        tiled=True,
    )
    out_part = sum_weight(dot_tn(hidden_wide, mixed))
    in_part = sum_weight(dot_tn(wide_one, d_mixer_in))
    own_cols = 3 * ffn_local + out_part.shape[1]
    own_sum = lax.psum(
        jnp.concatenate([ffn_part, out_part, in_part[:, :block_cols]], axis=1), "dp"
    ).astype(jnp.float32)
    shared_sum = lax.psum(in_part[:, block_cols:], ("dp", "col")).astype(jnp.float32)
    gate_up_sum = own_sum[:, : 2 * ffn_local]
    down_sum = own_sum[:, 2 * ffn_local : 3 * ffn_local].T
    outer_sum = own_sum[:, 3 * ffn_local : own_cols].T
    block_sum = own_sum[:, own_cols:]
    conv_sum, bias_sum, decay_sum, skip_sum, mixer_sum = lax.psum(
        (mixer_grads[1], mixer_grads[3], mixer_grads[4], mixer_grads[5], grad_gain_mix),
        ("dp", "row"),
    )
    state_sum, first_all, second_all = lax.psum(
        (mixer_grads[2], grad_first, grad_second), ("dp", "row", "col")
    )
    gain_at = lax.axis_index(("row", "col")) * gain_local
    first_sum = lax.dynamic_slice(first_all, (gain_at,), (gain_local,))
    second_sum = lax.dynamic_slice(second_all, (gain_at,), (gain_local,))
    first_col = 2 * inner_local
    return (
        leaving[0],
        leaving[1],
        first_sum,
        block_sum[:, :inner_local],
        block_sum[:, inner_local:first_col],
        block_sum[:, first_col : first_col + step_local],
        block_sum[:, first_col + step_local :],
        shared_sum[:, :state_cols],
        shared_sum[:, state_cols:],
        conv_sum,
        state_sum,
        bias_sum,
        decay_sum,
        skip_sum,
        mixer_sum,
        outer_sum[:inner_local],
        outer_sum[inner_local:],
        second_sum,
        gate_up_sum[:, :ffn_local],
        gate_up_sum[:, ffn_local:],
        down_sum,
    )


def solution(mesh):
    in_specs = (
        P("dp", ("row", "col")),
        P(("row", "col")),
        P("row", "col"),
        P("row", "col"),
        P("row", "col"),
        P("row", "col"),
        P("row", None),
        P("row", None),
        P(None, "col"),
        P(),
        P("col"),
        P("col"),
        P("col"),
        P("col"),
        P("col", "row"),
        P("col", "row"),
        P(("row", "col")),
        P("row", "col"),
        P("row", "col"),
        P("col", "row"),
        P("dp", ("row", "col")),
    )
    out_specs = (
        P("dp", ("row", "col")),
        P("dp", ("row", "col")),
        P(("row", "col")),
        P("row", "col"),
        P("row", "col"),
        P("row", "col"),
        P("row", "col"),
        P("row", None),
        P("row", None),
        P(None, "col"),
        P(),
        P("col"),
        P("col"),
        P("col"),
        P("col"),
        P("col", "row"),
        P("col", "row"),
        P(("row", "col")),
        P("row", "col"),
        P("row", "col"),
        P("col", "row"),
    )
    return jax.shard_map(
        on_device, mesh=mesh, in_specs=in_specs, out_specs=out_specs, check_vma=False
    )
```

time: 2300 us -> 900 us (0.39)
  waiting for transfers between devices: 1590 us -> 443 us
  blocking collectives: 325 us -> 122 us
  matrix products: 245 us -> 112 us
  local copies, waits for them, and re-layouts: 40.2 us -> 108 us
    reduce_scatter x8 -> x7, waiting for transfers between devices: 1060 us -> 256 us  [the longest x3 160 us: sum_weight(): lax.psum_scatter(partial_sum.astype(jnp.bfloat16), 'row', scatter_dimensi...]
    all_gather x8 -> x7, waiting for transfers between devices: 471 us -> 146 us  [the longest x4 74.6 us: gather_tokens(): return lax.all_gather(values, 'col', axis=0, tiled=True)]
    psum x9 -> x4, blocking collectives: 325 us -> 72.1 us  [the longest x1 38.7 us: on_device(): lax.psum((mixer_grads[2], grad_first, grad_second), ('dp', 'row', 'col'))]
    dot_general x12 -> x23, matrix products: 158 us -> 47.4 us  [the longest x21 47.1 us: batch_dot(): jnp.einsum(spec, left.astype(jnp.bfloat16), right.astype(jnp.bfloat16), p...]
    all_gather x0 -> x1, blocking collectives: none -> 50.2 us  [on_device(): lax.all_gather(jnp.stack([gain_first, gain_second]), ('row', 'col'), axis...]
    reshape x0 -> x20, local copies, waits for them, and re-layouts: none -> 28 us  [the longest x4 6.56 us: per_channel(): return wide.reshape(values.shape[:-1] + (values.shape[-1] * head_width,))]
    unnamed x214 -> x341, local copies, waits for them, and re-layouts: 15.6 us -> 41.9 us
  transfers between devices with their start and end apart: 18 -> 18, of which waited for: 14 -> 14; matrix products, arithmetic and copies ran while one was open for 10% -> 16% of each run, Pallas kernels for 0% -> 0%
where the time goes in v1:
time: 900 us; the launch traced here: 894 us
  waiting for transfers between devices  443 us (49%)
  blocking collectives  122 us (14%)
  matrix products  112 us (12%)
  local copies, waits for them, and re-layouts  108 us (12%)
  other arithmetic  79.7 us (9%)
  between operations  16.1 us (2%)
  starting transfers between devices  13.6 us (2%)
    reduce_scatter x3, waiting for transfers between devices, sum_weight(): lax.psum_scatter(partial_sum.astype(jnp.bfloat16), 'row', scatter_dimensi...  160 us
    reduce_scatter x4, waiting for transfers between devices, sum_tokens(): lax.psum_scatter(partial_sum.astype(jnp.bfloat16), 'col', scatter_dimensi...  96.1 us
    all_gather x4, waiting for transfers between devices, gather_tokens(): return lax.all_gather(values, 'col', axis=0, tiled=True)  74.6 us
    all_gather x3, waiting for transfers between devices, gather_rows(): return lax.all_gather(weight, 'row', axis=0, tiled=True)  71.6 us
    all_gather x1, blocking collectives, on_device(): lax.all_gather(jnp.stack([gain_first, gain_second]), ('row', 'col'), axis...  50.2 us
    dot_general x21, matrix products, batch_dot(): jnp.einsum(spec, left.astype(jnp.bfloat16), right.astype(jnp.bfloat16), p...  47.1 us
    unnamed x341, local copies, waits for them, and re-layouts  41.9 us
    psum x1, waiting for transfers between devices, on_device(): lax.psum(jnp.concatenate([ffn_part, out_part, in_part[:, :block_cols]], a...  39.9 us
  transfers between devices with their start and end apart: 18, of which 14 were waited for; matrix products, arithmetic and copies ran while one was open for 16% of the time, Pallas kernels for 0%

profile of v1, /device:TPU:0, one launch (start us, length us, event | category | flops | bytes accessed | tf_op | source)
XLA Modules:
  0.0 894.1 jit_solution(10959438551496596249)
XLA Ops:
  10.4 2.8 copy.425
  15.5 7.5 all-to-all-start
  23.1 50.2 %all-gather = f32[16,64,2]{1,2,0:T(2,128)S(1)} all-gather(f32[1,64,2]{1,2,0:T(2,128)S(1)} %maximum_bitcast_fusion.1), channel_id=1, replica_groups=mesh['dp'=2,'row'=4,'col'=4] {'row','col'}, dimensions={0}, use_global_device_ids=true | all-gather | bytes 8704 | tf_op jit(solution)/shard_map/all_gather | solution.py:225
  85.3 13.3 %all-gather.11.cloned.1.call-done = bf16[1024,1414]{1,0:T(8,128)(2,1)} async-done(((bf16[256,1414]{1,0:T(8,128)(2,1)}), bf16[1024,1414]{1,0:T(8,128)(2,1)}) %all-gather.11.cloned.1.call-update) | async-done | bytes 2895888 | tf_op jit(solution)/shard_map/all_gather | solution.py:38
  98.7 23.3 %all-gather.9.cloned.1.call-done = bf16[1024,1024]{1,0:T(8,128)(2,1)} async-done(((bf16[256,1024]{1,0:T(8,128)(2,1)}), bf16[1024,1024]{1,0:T(8,128)(2,1)}) %all-gather.9.cloned.1.call-update) | async-done | bytes 2097168 | tf_op jit(solution)/shard_map/all_gather | solution.py:42
  122.0 5.8 fusion.184
  131.7 4.4 multiply_convert_fusion.8
  137.5 2.7 convert_bitcast_fusion
  141.8 2.4 fusion.43
  144.2 3.0 copy.445
  148.6 3.1 copy.444
  156.3 2.8 multiply_add_fusion.1
  160.8 3.3 multiply_reduce_fusion.7
  164.1 6.1 psum.84
  174.5 8.5 fusion.185
  184.2 4.7 divide_convert_fusion
  191.8 4.2 convolution_convert_fusion.7
  200.1 28.5 %reduce-scatter.8.cloned.1.call-done = bf16[256,1024]{1,0:T(8,128)(2,1)} async-done(((bf16[1024,1024]{1,0:T(8,128)(2,1)}), bf16[256,1024]{1,0:T(8,128)(2,1)}) %reduce-scatter.8.cloned.1.call-update) | async-done | bytes 524304 | tf_op jit(solution)/shard_map/reduce_scatter | solution.py:46
  235.3 58.3 %all-gather.17.cloned.1.call-done = bf16[1024,1536]{0,1:T(8,128)(2,1)} async-done(((bf16[256,1536]{0,1:T(8,128)(2,1)}), bf16[1024,1536]{0,1:T(8,128)(2,1)}) %all-gather.17.cloned.1.call-update) | async-done | bytes 3145744 | tf_op jit(solution)/shard_map/all_gather | solution.py:38
  293.5 22.9 %all-gather.15.cloned.1.call-done = bf16[1024,1024]{1,0:T(8,128)(2,1)} async-done(((bf16[256,1024]{1,0:T(8,128)(2,1)}), bf16[1024,1024]{1,0:T(8,128)(2,1)}) %all-gather.15.cloned.1.call-update) | async-done | bytes 2097168 | tf_op jit(solution)/shard_map/all_gather | solution.py:42
  316.4 6.6 fusion.19
  323.0 18.5 %all-gather.19.cloned.1.call-done = bf16[1024,1024]{0,1:T(8,128)(2,1)} async-done(((bf16[256,1024]{0,1:T(8,128)(2,1)}), bf16[1024,1024]{0,1:T(8,128)(2,1)}) %all-gather.19.cloned.1.call-update) | async-done | bytes 2097168 | tf_op jit(solution)/shard_map/all_gather | solution.py:42
  341.5 6.2 multiply_convert_fusion.2
  349.1 3.8 convolution_convert_fusion.5
  353.0 4.2 convolution_convert_fusion.6
  359.3 25.3 %reduce-scatter.12.cloned.1.call-done = bf16[256,1024]{1,0:T(8,128)(2,1)} async-done(((bf16[1024,1024]{1,0:T(8,128)(2,1)}), bf16[256,1024]{1,0:T(8,128)(2,1)}) %reduce-scatter.12.cloned.1.call-update) | async-done | bytes 524304 | tf_op jit(solution)/shard_map/reduce_scatter | solution.py:46
  387.1 31.4 %reduce-scatter.10.cloned.1.call-done = bf16[256,1024]{1,0:T(8,128)(2,1)} async-done(((bf16[1024,1024]{1,0:T(8,128)(2,1)}), bf16[256,1024]{1,0:T(8,128)(2,1)}) %reduce-scatter.10.cloned.1.call-update) | async-done | bytes 524304 | tf_op jit(solution)/shard_map/reduce_scatter | solution.py:46
  418.5 2.8 fusion.81
  421.5 2.9 copy.543
  424.4 3.0 copy.489
  428.8 3.3 copy.483
  434.2 9.9 %all-gather.21.cloned.1.call-done = bf16[1024,1024]{1,0:T(8,128)(2,1)} async-done(((bf16[256,1024]{1,0:T(8,128)(2,1)}), bf16[1024,1024]{1,0:T(8,128)(2,1)}) %all-gather.21.cloned.1.call-update) | async-done | bytes 2097168 | tf_op jit(solution)/shard_map/all_gather | solution.py:42
  444.1 3.1 fusion.190
  451.1 4.5 fusion.56
  455.6 6.9 fusion.6
  462.6 5.2 convolution_convert_fusion.13
  467.7 5.4 fusion.59
  474.4 3.1 copy.534
  477.5 2.4 multiply_reduce_fusion
  479.9 6.6 psum.85
  487.2 6.0 multiply_reduce_fusion.1
  497.6 3.7 fusion.17
  501.2 2.7 fusion.40
  515.4 4.5 multiply_reduce_fusion.11
  523.6 3.2 copy.484
  526.8 4.5 convert_multiply_fusion.3
  533.5 3.2 copy.486
  536.7 2.7 mul.856
  541.5 3.1 copy.531
  544.6 7.1 multiply_reduce_fusion.5
  561.1 4.8 convolution_convert_fusion.4
  566.0 7.4 convolution_convert_fusion
  574.7 3.2 convolution_convert_fusion.10
  577.9 2.3 convolution_convert_fusion.3
  583.4 4.1 convolution_convert_fusion.9
  587.6 11.0 %reduce-scatter.14.cloned.1.call-done = bf16[256,1024]{1,0:T(8,128)(2,1)} async-done(((bf16[1024,1024]{1,0:T(8,128)(2,1)}), bf16[256,1024]{1,0:T(8,128)(2,1)}) %reduce-scatter.14.cloned.1.call-update) | async-done | bytes 524304 | tf_op jit(solution)/shard_map/reduce_scatter | solution.py:46
  603.2 4.7 all-to-all-start.1
  608.0 67.6 %reduce-scatter.20.cloned.1.call-done = bf16[256,1414]{0,1:T(8,128)(2,1)} async-done(((bf16[1024,1414]{0,1:T(8,128)(2,1)}), bf16[256,1414]{0,1:T(8,128)(2,1)}) %reduce-scatter.20.cloned.1.call-update) | async-done | bytes 723984 | tf_op jit(solution)/shard_map/reduce_scatter | solution.py:52
  677.6 63.2 %reduce-scatter.16.cloned.1.call-done = bf16[256,1536]{0,1:T(8,128)(2,1)} async-done(((bf16[1024,1536]{0,1:T(8,128)(2,1)}), bf16[256,1536]{0,1:T(8,128)(2,1)}) %reduce-scatter.16.cloned.1.call-update) | async-done | bytes 786448 | tf_op jit(solution)/shard_map/reduce_scatter | solution.py:52
  740.8 29.4 %reduce-scatter.18.cloned.1.call-done = bf16[256,512]{0,1:T(8,128)(2,1)} async-done(((bf16[1024,512]{0,1:T(8,128)(2,1)}), bf16[256,512]{0,1:T(8,128)(2,1)}) %reduce-scatter.18.cloned.1.call-update) | async-done | bytes 262160 | tf_op jit(solution)/shard_map/reduce_scatter | solution.py:52
  770.2 2.5 pad_maximum_fusion.2
  773.0 20.6 %all-reduce.42 = (f32[4,384]{1,0:T(4,128)}, f32[6]{0:T(128)}, f32[6]{0:T(128)}, f32[6]{0:T(128)}, f32[384]{0:T(512)}) all-reduce(f32[4,384]{1,0:T(4,128)S(1)} %pad_add_fusion.8, f32[6]{0:T(128)S(1)} %get-tuple-element.191, f32[6]{0:T(128)S(1)} %negate_multiply_fusion, ...), channel_id=1, replica_groups=mesh['dp'=2,'row'=4,'col'=4] {'dp','row'}, use_global_device_ids=true, to_apply=%region_41.42 | all-reduce | flops 1938 | bytes 15504 | tf_op jit(solution)/shard_map/psum | solution.py:333
  793.7 38.7 %all-reduce.41 = (f32[1024]{0:T(1024)S(1)}, f32[4,256]{1,0:T(4,128)}, f32[1024]{0:T(1024)S(1)}) all-reduce(f32[1024]{0:T(1024)S(1)} %get-tuple-element.165, f32[4,256]{1,0:T(4,128)S(1)} %pad_add_fusion.9, f32[1024]{0:T(1024)S(1)} %copy-done.111), channel_id=1, replica_groups=mesh['dp'=2,'row'=4,'col'=4] {'dp','row','col'}, use_global_device_ids=true, to_apply=%region_31.32 | all-reduce | flops 3072 | bytes 24576 | tf_op jit(solution)/shard_map/psum | solution.py:337
  838.2 39.9 %all-reduce.46.cloned.1.call-done = bf16[256,2950]{0,1:T(8,128)(2,1)} async-done(((bf16[256,2950]{0,1:T(8,128)(2,1)}), bf16[256,2950]{0,1:T(8,128)(2,1)}) %all-reduce.46.cloned.1.call-update) | async-done | bytes 1510416 | tf_op jit(solution)/shard_map/psum | solution.py:325
  (529 shorter events, 124.9 us)
Async XLA Ops:
  7.2 91.5 %all-gather.11.cloned.1.call-start = ((), (), s32[]{:S(2)}) async-start(), calls=%async_computation.10 | async-start | bytes 3932160 | tf_op jit(solution)/shard_map/all_gather | solution.py:38
  15.5 7.6 copy-start.142
  15.5 7.6 copy-start.143
  15.5 58.5 %all-to-all-start = ((bf16[16,2,16384]{2,1,0:T(2,128)(2,1)}), bf16[16,2,16384]{2,1,0:T(2,128)(2,1)S(1)}, u32[]{:S(2)}, u32[]{:S(2)}) async-start(bf16[16,2,16384]{2,1,0:T(2,128)(2,1)} %reshape.757), calls=%async_computation | async-start | bytes 2097152 | tf_op jit(solution)/shard_map/all_to_all | solution.py:218
  23.0 99.0 %all-gather.9.cloned.1.call-start = ((), (), s32[]{:S(2)}) async-start(), calls=%async_computation.9 | async-start | bytes 2621440 | tf_op jit(solution)/shard_map/all_gather | solution.py:42
  80.9 110.9 %all-gather.13.cloned.1.call-start = ((), (), s32[]{:S(2)}) async-start(), calls=%async_computation.11 | async-start | bytes 1310720 | tf_op jit(solution)/shard_map/all_gather | solution.py:38
  81.7 146.9 %reduce-scatter.8.cloned.1.call-start = ((), (), s32[]{:S(2)}) async-start(), calls=%async_computation.12 | async-start | bytes 2621440 | tf_op jit(solution)/shard_map/reduce_scatter | solution.py:46
  82.6 59.2 %copy-start.112 = (pred[128,128]{1,0:T(8,128)(4,1)}, pred[128,128]{1,0:T(8,128)(4,1)S(1)}, u32[]{:S(2)}) copy-start(pred[128,128]{1,0:T(8,128)(4,1)S(1)} %iota_compare_fusion.1) | copy-start | bytes 49156
  83.9 47.1 %copy-start.139 = (f32[6]{0:T(128)}, f32[6]{0:T(128)S(1)}, u32[]{:S(2)}) copy-start(f32[6]{0:T(128)S(1)} %exponential_negate_fusion) | copy-start | bytes 76
  84.0 53.4 %copy-start.101 = (f32[384]{0:T(512)}, f32[384]{0:T(512)S(1)}, u32[]{:S(2)}) copy-start(f32[384]{0:T(512)S(1)} %get-tuple-element.178) | copy-start | bytes 4612
  84.0 53.4 %copy-start.103 = (f32[384]{0:T(512)}, f32[384]{0:T(512)S(1)}, u32[]{:S(2)}) copy-start(f32[384]{0:T(512)S(1)} %get-tuple-element.179) | copy-start | bytes 4612
  84.0 53.4 %copy-start.105 = (f32[384]{0:T(512)}, f32[384]{0:T(512)S(1)}, u32[]{:S(2)}) copy-start(f32[384]{0:T(512)S(1)} %get-tuple-element.180) | copy-start | bytes 4612
  84.0 53.4 %copy-start.107 = (f32[384]{0:T(512)}, f32[384]{0:T(512)S(1)}, u32[]{:S(2)}) copy-start(f32[384]{0:T(512)S(1)} %get-tuple-element.177) | copy-start | bytes 4612
  84.0 47.6 %copy-start.116 = (f32[1,256]{1,0:T(1,128)}, f32[1,256]{1,0:T(1,128)S(1)}, u32[]{:S(2)}) copy-start(f32[1,256]{1,0:T(1,128)S(1)} %get-tuple-element.259) | copy-start | bytes 3076
  84.1 47.6 %copy-start.118 = (f32[1,256]{1,0:T(1,128)}, f32[1,256]{1,0:T(1,128)S(1)}, u32[]{:S(2)}) copy-start(f32[1,256]{1,0:T(1,128)S(1)} %get-tuple-element.260) | copy-start | bytes 3076
  84.1 47.6 %copy-start.120 = (f32[1,256]{1,0:T(1,128)}, f32[1,256]{1,0:T(1,128)S(1)}, u32[]{:S(2)}) copy-start(f32[1,256]{1,0:T(1,128)S(1)} %get-tuple-element.261) | copy-start | bytes 3076
  84.1 47.6 %copy-start.122 = (f32[1,256]{1,0:T(1,128)}, f32[1,256]{1,0:T(1,128)S(1)}, u32[]{:S(2)}) copy-start(f32[1,256]{1,0:T(1,128)S(1)} %get-tuple-element.262) | copy-start | bytes 3076
  128.1 9.4 %copy-start.6 = (f32[1024,384]{0,1:T(8,128)}, f32[1024,384]{0,1:T(8,128)S(1)}, u32[]{:S(2)}) copy-start(f32[1024,384]{0,1:T(8,128)S(1)} %slice.327) | copy-start | bytes 4718596
  131.4 10.4 %copy-start.94 = (f32[8,6,128]{2,1,0:T(8,128)}, f32[8,6,128]{2,1,0:T(8,128)S(1)}, u32[]{:S(2)}) copy-start(f32[8,6,128]{2,1,0:T(8,128)S(1)} %copy.431) | copy-start | bytes 73732
  136.2 20.1 %copy-start.14 = (bf16[16,8,8,128]{3,2,1,0:T(8,128)(2,1)}, bf16[16,8,8,128]{3,2,1,0:T(8,128)(2,1)S(1)}, u32[]{:S(2)}) copy-start(bf16[16,8,8,128]{3,2,1,0:T(8,128)(2,1)S(1)} %get-tuple-element.248) | copy-start | bytes 786436
  136.5 15.8 %copy-start.84 = (f32[384]{0:T(512)}, f32[384]{0:T(512)S(1)}, u32[]{:S(2)}) copy-start(f32[384]{0:T(512)S(1)} %broadcast_in_dim.185) | copy-start | bytes 4612
  136.7 15.6 %copy-start.82 = (f32[384]{0:T(512)}, f32[384]{0:T(512)S(1)}, u32[]{:S(2)}) copy-start(f32[384]{0:T(512)S(1)} %broadcast_in_dim.188) | copy-start | bytes 4612
  136.8 16.8 %copy-start.73 = (f32[384]{0:T(512)}, f32[384]{0:T(512)S(1)}, u32[]{:S(2)}) copy-start(f32[384]{0:T(512)S(1)} %broadcast_in_dim.190) | copy-start | bytes 4612
  137.0 16.7 %copy-start.75 = (f32[384]{0:T(512)}, f32[384]{0:T(512)S(1)}, u32[]{:S(2)}) copy-start(f32[384]{0:T(512)S(1)} %broadcast_in_dim.192) | copy-start | bytes 4612
  137.1 17.9 %copy-start.86 = (f32[384]{0:T(512)}, f32[384]{0:T(512)S(1)}, u32[]{:S(2)}) copy-start(f32[384]{0:T(512)S(1)} %broadcast_in_dim.194) | copy-start | bytes 4612
  137.3 17.7 %copy-start.88 = (f32[384]{0:T(512)}, f32[384]{0:T(512)S(1)}, u32[]{:S(2)}) copy-start(f32[384]{0:T(512)S(1)} %broadcast_in_dim.196) | copy-start | bytes 4612
  137.4 18.2 %copy-start.92 = (f32[384]{0:T(512)}, f32[384]{0:T(512)S(1)}, u32[]{:S(2)}) copy-start(f32[384]{0:T(512)S(1)} %broadcast_in_dim.198) | copy-start | bytes 4612
  141.3 14.4 %copy-start.3 = (f32[8,128,384]{2,1,0:T(8,128)}, f32[8,128,384]{2,1,0:T(8,128)S(1)}, u32[]{:S(2)}) copy-start(f32[8,128,384]{2,1,0:T(8,128)S(1)} %fusion.83) | copy-start | bytes 4718596
  160.8 10.0 %copy-start.70 = (bf16[1024,128]{0,1:T(8,128)(2,1)S(1)}, bf16[1024,128]{0,1:T(8,128)(2,1)}, u32[]{:S(2)}) copy-start(bf16[1024,128]{0,1:T(8,128)(2,1)} %get-tuple-element.227) | copy-start | bytes 786436
  174.5 8.5 copy-start.69
  196.0 97.6 %all-gather.17.cloned.1.call-start = ((), (), s32[]{:S(2)}) async-start(), calls=%async_computation.14 | async-start | bytes 3932160 | tf_op jit(solution)/shard_map/all_gather | solution.py:38
  200.1 116.3 %all-gather.15.cloned.1.call-start = ((), (), s32[]{:S(2)}) async-start(), calls=%async_computation.13 | async-start | bytes 2621440 | tf_op jit(solution)/shard_map/all_gather | solution.py:42
  232.7 108.7 %all-gather.19.cloned.1.call-start = ((), (), s32[]{:S(2)}) async-start(), calls=%async_computation.16 | async-start | bytes 2621440 | tf_op jit(solution)/shard_map/all_gather | solution.py:42
  234.8 149.7 %reduce-scatter.12.cloned.1.call-start = ((), (), s32[]{:S(2)}) async-start(), calls=%async_computation.17 | async-start | bytes 2621440 | tf_op jit(solution)/shard_map/reduce_scatter | solution.py:46
  341.5 7.6 copy-start.145
  352.9 65.6 %reduce-scatter.10.cloned.1.call-start = ((), (), s32[]{:S(2)}) async-start(), calls=%async_computation.15 | async-start | bytes 2621440 | tf_op jit(solution)/shard_map/reduce_scatter | solution.py:46
  357.2 86.9 %all-gather.21.cloned.1.call-start = ((), (), s32[]{:S(2)}) async-start(), calls=%async_computation.18 | async-start | bytes 2621440 | tf_op jit(solution)/shard_map/all_gather | solution.py:42
  421.3 177.2 %reduce-scatter.14.cloned.1.call-start = ((), (), s32[]{:S(2)}) async-start(), calls=%async_computation.19 | async-start | bytes 2621440 | tf_op jit(solution)/shard_map/reduce_scatter | solution.py:46
  451.1 11.4 %slice-start = ((s8[8388608]{0:T(1024)(128)(4,1)}), s8[4194304]{0:T(1024)(128)(4,1)S(1)}, s32[]{:S(2)}) async-start(s8[8388608]{0:T(1024)(128)(4,1)} %bitcast.326), calls=%async_computation.25 | async-start | bytes 8388608
  477.5 9.0 %copy-start.91 = (f32[1024]{0:T(1024)S(1)}, f32[1024]{0:T(1024)}, u32[]{:S(2)}) copy-start(f32[1024]{0:T(1024)} %copy-done.90) | copy-start | bytes 12292
  477.5 9.7 %copy-start.97 = (f32[384]{0:T(512)S(1)}, f32[384]{0:T(512)}, u32[]{:S(2)}) copy-start(f32[384]{0:T(512)} %mul.795) | copy-start | bytes 4612
  565.9 109.7 %reduce-scatter.20.cloned.1.call-start = ((), (), s32[]{:S(2)}) async-start(), calls=%async_computation.22 | async-start | bytes 3624960 | tf_op jit(solution)/shard_map/reduce_scatter | solution.py:52
  573.4 167.4 %reduce-scatter.16.cloned.1.call-start = ((), (), s32[]{:S(2)}) async-start(), calls=%async_computation.20 | async-start | bytes 3932160 | tf_op jit(solution)/shard_map/reduce_scatter | solution.py:52
  582.2 16.3 %copy-start.81 = (f32[1,1024]{1,0:T(1,128)S(1)}, f32[1,1024]{1,0:T(1,128)}, u32[]{:S(2)}) copy-start(f32[1,1024]{1,0:T(1,128)} %copy-done.80) | copy-start | bytes 12292
  582.3 16.3 %copy-start.115 = (f32[256]{0:T(256)S(1)}, f32[256]{0:T(256)}, u32[]{:S(2)}) copy-start(f32[256]{0:T(256)} %copy-done.114) | copy-start | bytes 3076
  582.3 187.9 %reduce-scatter.18.cloned.1.call-start = ((), (), s32[]{:S(2)}) async-start(), calls=%async_computation.21 | async-start | bytes 1310720 | tf_op jit(solution)/shard_map/reduce_scatter | solution.py:52
  587.5 12.5 %copy-start.126 = (f32[256]{0:T(256)S(1)}, f32[256]{0:T(256)}, u32[]{:S(2)}) copy-start(f32[256]{0:T(256)} %copy-done.125) | copy-start | bytes 3076
  587.5 12.5 %copy-start.23 = (bf16[256,1024]{1,0:T(8,128)(2,1)S(1)}, bf16[256,1024]{1,0:T(8,128)(2,1)}, u32[]{:S(2)}) copy-start(bf16[256,1024]{1,0:T(8,128)(2,1)} %reduce-scatter.12.cloned.1.call-done) | copy-start | bytes 1572868
  587.5 12.5 %copy-start.24 = (bf16[256,1024]{1,0:T(8,128)(2,1)S(1)}, bf16[256,1024]{1,0:T(8,128)(2,1)}, u32[]{:S(2)}) copy-start(bf16[256,1024]{1,0:T(8,128)(2,1)} %copy.458) | copy-start | bytes 1572868
  587.5 12.5 %copy-start.72 = (f32[1,1024]{1,0:T(1,128)S(1)}, f32[1,1024]{1,0:T(1,128)}, u32[]{:S(2)}) copy-start(f32[1,1024]{1,0:T(1,128)} %get-tuple-element.257) | copy-start | bytes 12292
  587.5 12.5 %copy-start.100 = (f32[256]{0:T(256)S(1)}, f32[256]{0:T(256)}, u32[]{:S(2)}) copy-start(f32[256]{0:T(256)} %copy-done.99) | copy-start | bytes 3076
  587.5 12.5 %copy-start.124 = (f32[256]{0:T(256)S(1)}, f32[256]{0:T(256)}, u32[]{:S(2)}) copy-start(f32[256]{0:T(256)} %fusion.147) | copy-start | bytes 3076
  603.2 233.0 %all-to-all-start.1 = ((bf16[2,256,1024]{1,0,2:T(2,128)(2,1)}), bf16[2,256,1024]{1,0,2:T(2,128)(2,1)S(1)}, u32[]{:S(2)}, u32[]{:S(2)}) async-start(bf16[2,256,1024]{1,0,2:T(2,128)(2,1)} %copy.499), calls=%async_computation.5 | async-start | bytes 2097152 | tf_op jit(solution)/shard_map/all_to_all | solution.py:315
  608.0 225.6 %all-reduce.48.cloned.1.call-start = ((), (), s32[]{:S(2)}) async-start(), calls=%async_computation.24 | async-start | bytes 524288 | tf_op jit(solution)/shard_map/psum | solution.py:328
  675.7 94.5 %slice-start.2 = ((bf16[256,1414]{0,1:T(8,128)(2,1)}), bf16[256,902]{0,1:T(8,128)(2,1)S(1)}, s32[]{:S(2)}) async-start(bf16[256,1414]{0,1:T(8,128)(2,1)} %reduce-scatter.20.cloned.1.call-done), calls=%async_computation.27 | async-start | bytes 925696 | tf_op jit(solution)/shard_map/slice | solution.py:326
  677.5 200.6 %all-reduce.46.cloned.1.call-start = ((), (), s32[]{:S(2)}) async-start(), calls=%async_computation.23 | async-start | bytes 3022848 | tf_op jit(solution)/shard_map/psum | solution.py:325
  677.5 95.2 %copy-start.130 = (f32[384]{0:T(512)S(1)}, f32[384]{0:T(512)}, u32[]{:S(2)}) copy-start(f32[384]{0:T(512)} %get-tuple-element.189) | copy-start | bytes 4612
  677.5 95.5 %copy-start.148 = (f32[6]{0:T(128)S(1)}, f32[6]{0:T(128)}, u32[]{:S(2)}) copy-start(f32[6]{0:T(128)} %param.32) | copy-start | bytes 76
  677.5 95.5 %copy-start.129 = (f32[384]{0:T(512)S(1)}, f32[384]{0:T(512)}, u32[]{:S(2)}) copy-start(f32[384]{0:T(512)} %get-tuple-element.151) | copy-start | bytes 4612
  677.6 116.1 %copy-start.132 = (f32[256]{0:T(256)S(1)}, f32[256]{0:T(256)}, u32[]{:S(2)}) copy-start(f32[256]{0:T(256)} %get-tuple-element.160) | copy-start | bytes 3076
  677.6 116.1 %copy-start.133 = (f32[256]{0:T(256)S(1)}, f32[256]{0:T(256)}, u32[]{:S(2)}) copy-start(f32[256]{0:T(256)} %get-tuple-element.161) | copy-start | bytes 3076
  677.6 116.1 %copy-start.134 = (f32[256]{0:T(256)S(1)}, f32[256]{0:T(256)}, u32[]{:S(2)}) copy-start(f32[256]{0:T(256)} %get-tuple-element.162) | copy-start | bytes 3076
  677.6 116.1 %copy-start.135 = (f32[256]{0:T(256)S(1)}, f32[256]{0:T(256)}, u32[]{:S(2)}) copy-start(f32[256]{0:T(256)} %get-tuple-element.167) | copy-start | bytes 3076
  677.6 116.1 %copy-start.111 = (f32[1024]{0:T(1024)S(1)}, f32[1024]{0:T(1024)}, u32[]{:S(2)}) copy-start(f32[1024]{0:T(1024)} %get-tuple-element.158) | copy-start | bytes 12292
  (115 other events, 299.0 us)
Sparse Core Ops, SparseCore 0:
  10.4 88.2 all-gather.10
  100.8 21.1 all-gather.8
  124.2 30.1 all-gather.12
  196.1 32.4 reduce-scatter.7
  230.1 63.4 all-gather.16
  295.6 20.7 all-gather.14
  318.6 22.8 all-gather.18
  353.0 31.4 reduce-scatter.11
  387.0 31.4 reduce-scatter.9
  421.4 22.5 all-gather.20
  566.0 32.4 reduce-scatter.13
  600.7 74.9 reduce-scatter.19
  678.0 62.8 reduce-scatter.15
  743.0 27.1 reduce-scatter.17
  774.0 52.3 all-reduce.47
  828.5 49.5 all-reduce.45

commit v2 on v1

--- a/solution.py
+++ b/solution.py
@@ -231,13 +231,14 @@
         )
     )
     kernel_out = gather_rows(jnp.concatenate([out_mamba, out_attn], axis=0).T)
-    kernel_ffn = gather_rows(jnp.concatenate([ffn_gate, ffn_up, ffn_down.T], axis=1))
-    kernel_gate_up = kernel_ffn[:, : 2 * ffn_local]
-    kernel_down = kernel_ffn[:, 2 * ffn_local :]
 
     residual = entering[0].astype(jnp.float32)
     normed_one, scale_one = norm_apply(residual, gains[0])
     wide_one = gather_tokens(normed_one.astype(jnp.bfloat16))
+    ffn_block, wide_one = lax.optimization_barrier(
+        (jnp.concatenate([ffn_gate, ffn_up, ffn_down.T], axis=1), wide_one)
+    )
+    kernel_ffn = gather_rows(ffn_block)
     mixer_in = plain_dot(wide_one, kernel_in).astype(jnp.bfloat16)
     seq_count = mixer_in.shape[0] // SEQ_LEN
 
@@ -269,6 +270,9 @@
     gated_scale = lax.rsqrt(lax.psum(jnp.sum(gated * gated, axis=1), "col") / DI + EPS)
     gated_norm = gated * gated_scale[:, None] * mixer_gain
     mixed = jnp.concatenate([gated_norm, attended], axis=1).astype(jnp.bfloat16)
+    mixed, kernel_ffn = lax.optimization_barrier((mixed, kernel_ffn))
+    kernel_gate_up = kernel_ffn[:, : 2 * ffn_local]
+    kernel_down = kernel_ffn[:, 2 * ffn_local :]
     hidden = residual + sum_tokens(dot_nt(mixed, kernel_out))
     normed_two, scale_two = norm_apply(hidden, gains[1])
     wide_two = gather_tokens(normed_two.astype(jnp.bfloat16))
@@ -283,10 +287,10 @@
     d_up = d_active * gate_val * sigmoid_gate
     d_gate_up = jnp.concatenate([d_gate, d_up], axis=1).astype(jnp.bfloat16)
     d_normed_two = sum_tokens(dot_nt(d_gate_up, kernel_gate_up))
-    ffn_part = sum_weight(
-        jnp.concatenate([dot_tn(wide_two, d_gate_up), dot_tn(out_wide, active)], axis=1)
-    )
-    block_out = (hidden + sum_tokens(dot_nt(active, kernel_down))).astype(jnp.bfloat16)
+    ffn_grads = jnp.concatenate(
+        [dot_tn(wide_two, d_gate_up), dot_tn(out_wide, active)], axis=1
+    ).astype(jnp.bfloat16)
+    block_partial = dot_nt(active, kernel_down).astype(jnp.bfloat16)
 
     def whole_row(values):
         return values
@@ -296,7 +300,13 @@
     )
     d_hidden = entering[1].astype(jnp.float32) + d_hidden_norm
     hidden_wide = gather_tokens(d_hidden.astype(jnp.bfloat16))
+    ffn_grads, block_partial, hidden_wide = lax.optimization_barrier(
+        (ffn_grads, block_partial, hidden_wide)
+    )
     d_mixed = plain_dot(hidden_wide, kernel_out)
+    block_out = (hidden + sum_tokens(block_partial)).astype(jnp.bfloat16)
+    ffn_part = sum_weight(ffn_grads)
+    out_part = sum_weight(dot_tn(hidden_wide, mixed))
     d_gated, grad_gain_mix = norm_back(
         gated,
         gated_scale,
@@ -306,7 +316,9 @@
         lambda values: lax.psum(values, "col"),
     )
     mixer_grads = pull((d_gated, d_mixed[:, inner_local:]))
-    d_mixer_in = mixer_grads[0].astype(jnp.bfloat16)
+    d_mixer_in, block_out, ffn_part, out_part = lax.optimization_barrier(
+        (mixer_grads[0].astype(jnp.bfloat16), block_out, ffn_part, out_part)
+    )
     d_normed_one = sum_tokens(dot_nt(d_mixer_in, kernel_in))
     d_tokens_norm, grad_first = norm_back(
         residual, scale_one, gains[0], d_normed_one, D, whole_row
@@ -319,24 +331,42 @@
         concat_axis=1,
         tiled=True,
     )
-    out_part = sum_weight(dot_tn(hidden_wide, mixed))
     in_part = sum_weight(dot_tn(wide_one, d_mixer_in))
-    own_cols = 3 * ffn_local + out_part.shape[1]
-    own_sum = lax.psum(
-        jnp.concatenate([ffn_part, out_part, in_part[:, :block_cols]], axis=1), "dp"
-    ).astype(jnp.float32)
+    own_sum = lax.psum(jnp.concatenate([ffn_part, out_part], axis=1), "dp").astype(jnp.float32)
+    block_sum = lax.psum(in_part[:, :block_cols], "dp").astype(jnp.float32)
     shared_sum = lax.psum(in_part[:, block_cols:], ("dp", "col")).astype(jnp.float32)
     gate_up_sum = own_sum[:, : 2 * ffn_local]
     down_sum = own_sum[:, 2 * ffn_local : 3 * ffn_local].T
-    outer_sum = own_sum[:, 3 * ffn_local : own_cols].T
-    block_sum = own_sum[:, own_cols:]
-    conv_sum, bias_sum, decay_sum, skip_sum, mixer_sum = lax.psum(
-        (mixer_grads[1], mixer_grads[3], mixer_grads[4], mixer_grads[5], grad_gain_mix),
-        ("dp", "row"),
-    )
-    state_sum, first_all, second_all = lax.psum(
-        (mixer_grads[2], grad_first, grad_second), ("dp", "row", "col")
-    )
+    outer_sum = own_sum[:, 3 * ffn_local :].T
+    col_count = lax.axis_size("col")
+    col_at = lax.axis_index("col")
+    own_small = jnp.concatenate(
+        [
+            mixer_grads[1].reshape(-1),
+            mixer_grads[3],
+            mixer_grads[4],
+            mixer_grads[5],
+            grad_gain_mix,
+        ]
+    )
+    slots = jnp.where(jnp.arange(col_count)[:, None] == col_at, own_small[None, :], 0.0)
+    small = lax.psum(
+        jnp.concatenate(
+            [slots.reshape(-1), mixer_grads[2].reshape(-1), grad_first, grad_second]
+        ),
+        ("dp", "row", "col"),
+    )
+    own_size = own_small.shape[0]
+    own_all = lax.dynamic_slice(small, (col_at * own_size,), (own_size,))
+    cuts = [conv_inner.size]
+    for count in (step_local, step_local, step_local):
+        cuts.append(cuts[-1] + count)
+    conv_sum, bias_sum, decay_sum, skip_sum, mixer_sum = jnp.split(own_all, cuts)
+    conv_sum = conv_sum.reshape(conv_inner.shape)
+    rest = small[col_count * own_size :]
+    state_sum = rest[: conv_state.size].reshape(conv_state.shape)
+    first_all = rest[conv_state.size : conv_state.size + D]
+    second_all = rest[conv_state.size + D :]
     gain_at = lax.axis_index(("row", "col")) * gain_local
     first_sum = lax.dynamic_slice(first_all, (gain_at,), (gain_local,))
     second_sum = lax.dynamic_slice(second_all, (gain_at,), (gain_local,))

time: 900 us -> 801 us (0.89)
  waiting for transfers between devices: 443 us -> 363 us
  blocking collectives: 122 us -> 91.6 us
  other arithmetic: 79.7 us -> 89.6 us
    reduce_scatter x3, waiting for transfers between devices: 160 us -> 67.7 us  [sum_weight(): lax.psum_scatter(partial_sum.astype(jnp.bfloat16), 'row', scatter_dimensi...]
    all_gather x1, blocking collectives: 50.2 us -> 33.4 us  [on_device(): lax.all_gather(jnp.stack([gain_first, gain_second]), ('row', 'col'), axis...]
    psum x2 -> x1, blocking collectives: 59.4 us -> 44.3 us  [on_device(): lax.psum(jnp.concatenate([slots.reshape(-1), mixer_grads[2].reshape(-1),...]
    all_gather x3, waiting for transfers between devices: 71.6 us -> 83.4 us  [gather_rows(): return lax.all_gather(weight, 'row', axis=0, tiled=True)]
    reduce_scatter x4, waiting for transfers between devices: 96.1 us -> 84.4 us  [sum_tokens(): lax.psum_scatter(partial_sum.astype(jnp.bfloat16), 'col', scatter_dimensi...]
    unnamed x341 -> x314, local copies, waits for them, and re-layouts: 41.9 us -> 30.4 us
  transfers between devices with their start and end apart: 18 -> 18, of which waited for: 14 -> 12; matrix products, arithmetic and copies ran while one was open for 16% -> 31% of each run, Pallas kernels for 0% -> 0%
where the time goes in v2:
time: 801 us; the launch traced here: 795 us
  waiting for transfers between devices  363 us (45%)
  matrix products  120 us (15%)
  local copies, waits for them, and re-layouts  101 us (13%)
  blocking collectives  91.6 us (11%)
  other arithmetic  89.6 us (11%)
  between operations  16 us (2%)
  starting transfers between devices  14.4 us (2%)
    reduce_scatter x4, waiting for transfers between devices, sum_tokens(): lax.psum_scatter(partial_sum.astype(jnp.bfloat16), 'col', scatter_dimensi...  84.4 us
    all_gather x3, waiting for transfers between devices, gather_rows(): return lax.all_gather(weight, 'row', axis=0, tiled=True)  83.4 us
    all_gather x4, waiting for transfers between devices, gather_tokens(): return lax.all_gather(values, 'col', axis=0, tiled=True)  70.9 us
    reduce_scatter x3, waiting for transfers between devices, sum_weight(): lax.psum_scatter(partial_sum.astype(jnp.bfloat16), 'row', scatter_dimensi...  67.7 us
    dot_general x21, matrix products, batch_dot(): jnp.einsum(spec, left.astype(jnp.bfloat16), right.astype(jnp.bfloat16), p...  54.6 us
    psum x1, waiting for transfers between devices, on_device(): block_sum = lax.psum(in_part[:, :block_cols], 'dp').astype(jnp.float32)  48.1 us
    psum x1, blocking collectives, on_device(): lax.psum(jnp.concatenate([slots.reshape(-1), mixer_grads[2].reshape(-1),...  44.3 us
    all_gather x1, blocking collectives, on_device(): lax.all_gather(jnp.stack([gain_first, gain_second]), ('row', 'col'), axis...  33.4 us
  transfers between devices with their start and end apart: 18, of which 12 were waited for; matrix products, arithmetic and copies ran while one was open for 31% of the time, Pallas kernels for 0%

profile of v2, /device:TPU:0, one launch (start us, length us, event | category | flops | bytes accessed | tf_op | source)
XLA Modules:
  0.0 795.1 jit_solution(9977464391144294235)
XLA Ops:
  8.5 2.8 copy.425
  11.3 2.3 reshape.784
  13.6 7.5 all-to-all-start
  21.2 33.4 %all-gather = f32[16,64,2]{1,2,0:T(2,128)S(1)} all-gather(f32[1,64,2]{1,2,0:T(2,128)S(1)} %maximum_bitcast_fusion.1), channel_id=1, replica_groups=mesh['dp'=2,'row'=4,'col'=4] {'row','col'}, dimensions={0}, use_global_device_ids=true | all-gather | bytes 8704 | tf_op jit(solution)/shard_map/all_gather | solution.py:225
  64.0 21.1 %all-gather.9.cloned.1.call-done = bf16[1024,1024]{1,0:T(8,128)(2,1)} async-done(((bf16[256,1024]{1,0:T(8,128)(2,1)}), bf16[1024,1024]{1,0:T(8,128)(2,1)}) %all-gather.9.cloned.1.call-update) | async-done | bytes 2097168 | tf_op jit(solution)/shard_map/all_gather | solution.py:42
  89.9 60.3 %all-gather.11.cloned.1.call-done = bf16[1024,1414]{1,0:T(8,128)(2,1)} async-done(((bf16[256,1414]{1,0:T(8,128)(2,1)}), bf16[1024,1414]{1,0:T(8,128)(2,1)}) %all-gather.11.cloned.1.call-update) | async-done | bytes 2895888 | tf_op jit(solution)/shard_map/all_gather | solution.py:38
  150.2 5.8 fusion.183
  160.0 4.5 multiply_convert_fusion.8
  165.8 2.7 convert_bitcast_fusion
  170.2 2.4 fusion.43
  172.5 3.0 copy.447
  176.9 3.1 copy.446
  184.6 2.7 multiply_add_fusion.1
  189.0 3.3 multiply_reduce_fusion.7
  192.3 7.1 psum.42
  203.7 8.5 %fusion.184 = (f32[2,1024]{1,0:T(2,128)}, f32[2,1024,1024]{1,2,0:T(8,128)}) fusion(pred[1024,1024]{0,1:T(8,128)(4,1)} %iota_compare_fusion, bf16[1024,2,64]{0,2,1:T(8,128)(2,1)S(1)} %bitcast.378, bf16[1024,2,64]{0,1,2:T(2,128)(2,1)} %fusion.55), kind=kOutput, calls=%fused_computation.362 | convolution fusion | flops 276825088 | bytes 9969664 | tf_op jit(solution)/shard_map/jvp()/sub | solution.py:179
  213.3 4.8 divide_convert_fusion
  221.2 23.1 %all-gather.15.cloned.1.call-done = bf16[1024,512]{0,1:T(8,128)(2,1)} async-done(((bf16[256,512]{0,1:T(8,128)(2,1)}), bf16[1024,512]{0,1:T(8,128)(2,1)}) %all-gather.15.cloned.1.call-update) | async-done | bytes 1048592 | tf_op jit(solution)/shard_map/all_gather | solution.py:38
  244.3 4.2 convolution_convert_fusion.7
  248.5 29.8 %reduce-scatter.8.cloned.1.call-done = bf16[256,1024]{1,0:T(8,128)(2,1)} async-done(((bf16[1024,1024]{1,0:T(8,128)(2,1)}), bf16[256,1024]{1,0:T(8,128)(2,1)}) %reduce-scatter.8.cloned.1.call-update) | async-done | bytes 524304 | tf_op jit(solution)/shard_map/reduce_scatter | solution.py:46
  284.8 20.4 %all-gather.17.cloned.1.call-done = bf16[1024,1024]{1,0:T(8,128)(2,1)} async-done(((bf16[256,1024]{1,0:T(8,128)(2,1)}), bf16[1024,1024]{1,0:T(8,128)(2,1)}) %all-gather.17.cloned.1.call-update) | async-done | bytes 2097168 | tf_op jit(solution)/shard_map/all_gather | solution.py:42
  305.2 6.6 fusion.19
  311.8 18.5 %all-gather.19.cloned.1.call-done = bf16[1024,1024]{0,1:T(8,128)(2,1)} async-done(((bf16[256,1024]{0,1:T(8,128)(2,1)}), bf16[1024,1024]{0,1:T(8,128)(2,1)}) %all-gather.19.cloned.1.call-update) | async-done | bytes 2097168 | tf_op jit(solution)/shard_map/all_gather | solution.py:42
  330.3 6.2 multiply_convert_fusion.3
  337.9 3.8 convolution_convert_fusion.5
  343.8 29.5 %reduce-scatter.10.cloned.1.call-done = bf16[256,1024]{1,0:T(8,128)(2,1)} async-done(((bf16[1024,1024]{1,0:T(8,128)(2,1)}), bf16[256,1024]{1,0:T(8,128)(2,1)}) %reduce-scatter.10.cloned.1.call-update) | async-done | bytes 524304 | tf_op jit(solution)/shard_map/reduce_scatter | solution.py:46
  377.2 4.1 convolution_convert_fusion.6
  381.4 3.4 convolution_convert_fusion.10
  384.8 2.3 convolution_convert_fusion.3
  389.1 10.8 %all-gather.21.cloned.1.call-done = bf16[1024,1024]{1,0:T(8,128)(2,1)} async-done(((bf16[256,1024]{1,0:T(8,128)(2,1)}), bf16[1024,1024]{1,0:T(8,128)(2,1)}) %all-gather.21.cloned.1.call-update) | async-done | bytes 2097168 | tf_op jit(solution)/shard_map/all_gather | solution.py:42
  400.5 2.9 copy.543
  403.3 3.1 copy.489
  407.7 3.1 copy.483
  412.9 3.1 fusion.189
  419.9 6.9 fusion.6
  427.4 3.1 copy.534
  430.5 2.4 multiply_reduce_fusion
  432.8 6.8 psum.43
  440.9 3.8 fusion.56
  445.9 2.2 convolution_convert_fusion.9
  448.1 6.5 multiply_reduce_fusion.1
  454.7 7.7 fusion.59
  467.8 3.7 fusion.17
  489.1 4.1 fusion.40
  493.3 3.0 copy.484
  496.3 5.1 convert_multiply_fusion.3
  501.4 3.1 copy.490
  506.2 3.1 copy.486
  509.3 3.2 mul.859
  512.5 3.0 copy.487
  517.2 3.0 copy.531
  520.2 7.2 multiply_reduce_fusion.5
  530.5 2.8 multiply_reduce_fusion.11
  534.5 2.3 fusion.73
  539.4 5.5 convolution_convert_fusion.13
  545.0 3.1 add_convert_fusion
  549.4 7.6 convolution_convert_fusion.4
  557.0 7.2 convolution_convert_fusion
  564.3 25.1 %reduce-scatter.18.cloned.1.call-done = bf16[256,1024]{1,0:T(8,128)(2,1)} async-done(((bf16[1024,1024]{1,0:T(8,128)(2,1)}), bf16[256,1024]{1,0:T(8,128)(2,1)}) %reduce-scatter.18.cloned.1.call-update) | async-done | bytes 524304 | tf_op jit(solution)/shard_map/reduce_scatter | solution.py:46
  593.7 4.8 all-to-all-start.1
  598.9 67.7 %reduce-scatter.20.cloned.1.call-done = bf16[256,1414]{0,1:T(8,128)(2,1)} async-done(((bf16[1024,1414]{0,1:T(8,128)(2,1)}), bf16[256,1414]{0,1:T(8,128)(2,1)}) %reduce-scatter.20.cloned.1.call-update) | async-done | bytes 723984 | tf_op jit(solution)/shard_map/reduce_scatter | solution.py:52
  670.8 44.3 %psum.44 = f32[10824]{0:T(1024)S(1)} all-reduce(f32[10824]{0:T(1024)S(1)} %concatenate.45), channel_id=1, replica_groups=mesh['dp'=2,'row'=4,'col'=4] {'dp','row','col'}, use_global_device_ids=true, to_apply=%region_47.48 | all-reduce | flops 10824 | bytes 86592 | tf_op jit(solution)/shard_map/psum | solution.py:353
  718.9 7.7 all-reduce.45.cloned.1.call-done
  731.2 48.1 %all-reduce.47.cloned.1.call-done = (bf16[256,902]{0,1:T(8,128)(2,1)}, bf16[256,2048]{0,1:T(8,128)(2,1)}) async-done(((bf16[256,902]{0,1:T(8,128)(2,1)}, bf16[256,2048]{0,1:T(8,128)(2,1)}), (bf16[256,902]{0,1:T(8,128)(2,1)}, bf16[256,2048]{0,1:T(8,128)(2,1)})) %all-reduce.47.cloned.1.call-update) | async-done | bytes 1510416 | tf_op jit(solution)/shard_map/psum | solution.py:336
  (515 shorter events, 124.7 us)
Async XLA Ops:
  13.6 7.6 copy-start.131
  13.6 7.6 copy-start.132
  13.6 41.7 %all-to-all-start = ((bf16[16,2,16384]{2,1,0:T(2,128)(2,1)}), bf16[16,2,16384]{2,1,0:T(2,128)(2,1)S(1)}, u32[]{:S(2)}, u32[]{:S(2)}) async-start(bf16[16,2,16384]{2,1,0:T(2,128)(2,1)} %reshape.784), calls=%async_computation | async-start | bytes 2097152 | tf_op jit(solution)/shard_map/all_to_all | solution.py:218
  21.1 64.0 %all-gather.9.cloned.1.call-start = ((), (), s32[]{:S(2)}) async-start(), calls=%async_computation.9 | async-start | bytes 2621440 | tf_op jit(solution)/shard_map/all_gather | solution.py:42
  61.2 89.0 %all-gather.11.cloned.1.call-start = ((), (), s32[]{:S(2)}) async-start(), calls=%async_computation.10 | async-start | bytes 3932160 | tf_op jit(solution)/shard_map/all_gather | solution.py:38
  62.7 158.5 %all-gather.13.cloned.1.call-start = ((), (), s32[]{:S(2)}) async-start(), calls=%async_computation.11 | async-start | bytes 3932160 | tf_op jit(solution)/shard_map/all_gather | solution.py:38
  62.9 22.3 %copy-start.53 = (bf16[384,256]{1,0:T(8,128)(2,1)S(1)}, bf16[384,256]{1,0:T(8,128)(2,1)}, u32[]{:S(2)}) copy-start(bf16[384,256]{1,0:T(8,128)(2,1)} %param.35) | copy-start | bytes 589828
  62.9 22.3 %copy-start.65 = (bf16[128,256]{1,0:T(8,128)(2,1)S(1)}, bf16[128,256]{1,0:T(8,128)(2,1)}, u32[]{:S(2)}) copy-start(bf16[128,256]{1,0:T(8,128)(2,1)} %param.36) | copy-start | bytes 196612
  64.0 24.5 %copy-start.136 = (f32[6]{0:T(128)S(1)}, f32[6]{0:T(128)}, u32[]{:S(2)}) copy-start(f32[6]{0:T(128)} %param.32) | copy-start | bytes 76
  64.0 24.5 %copy-start.123 = (f32[4,384]{1,0:T(4,128)S(1)}, f32[4,384]{1,0:T(4,128)}, u32[]{:S(2)}) copy-start(f32[4,384]{1,0:T(4,128)} %param.29) | copy-start | bytes 18436
  64.0 24.6 %copy-start.125 = (f32[4,256]{1,0:T(4,128)S(1)}, f32[4,256]{1,0:T(4,128)}, u32[]{:S(2)}) copy-start(f32[4,256]{1,0:T(4,128)} %param.30) | copy-start | bytes 12292
  64.0 24.6 %copy-start.130 = (f32[6]{0:T(128)S(1)}, f32[6]{0:T(128)}, u32[]{:S(2)}) copy-start(f32[6]{0:T(128)} %param.33) | copy-start | bytes 76
  85.1 159.2 %all-gather.15.cloned.1.call-start = ((), (), s32[]{:S(2)}) async-start(), calls=%async_computation.12 | async-start | bytes 1310720 | tf_op jit(solution)/shard_map/all_gather | solution.py:38
  85.9 192.4 %reduce-scatter.8.cloned.1.call-start = ((), (), s32[]{:S(2)}) async-start(), calls=%async_computation.13 | async-start | bytes 2621440 | tf_op jit(solution)/shard_map/reduce_scatter | solution.py:46
  87.2 83.0 %copy-start.102 = (pred[128,128]{1,0:T(8,128)(4,1)}, pred[128,128]{1,0:T(8,128)(4,1)S(1)}, u32[]{:S(2)}) copy-start(pred[128,128]{1,0:T(8,128)(4,1)S(1)} %iota_compare_fusion.1) | copy-start | bytes 49156
  88.5 70.8 %copy-start.128 = (f32[6]{0:T(128)}, f32[6]{0:T(128)S(1)}, u32[]{:S(2)}) copy-start(f32[6]{0:T(128)S(1)} %exponential_negate_fusion) | copy-start | bytes 76
  88.6 77.2 %copy-start.89 = (f32[384]{0:T(512)}, f32[384]{0:T(512)S(1)}, u32[]{:S(2)}) copy-start(f32[384]{0:T(512)S(1)} %get-tuple-element.200) | copy-start | bytes 4612
  88.6 77.2 %copy-start.91 = (f32[384]{0:T(512)}, f32[384]{0:T(512)S(1)}, u32[]{:S(2)}) copy-start(f32[384]{0:T(512)S(1)} %get-tuple-element.201) | copy-start | bytes 4612
  88.6 77.2 %copy-start.93 = (f32[384]{0:T(512)}, f32[384]{0:T(512)S(1)}, u32[]{:S(2)}) copy-start(f32[384]{0:T(512)S(1)} %get-tuple-element.202) | copy-start | bytes 4612
  88.6 77.2 %copy-start.95 = (f32[384]{0:T(512)}, f32[384]{0:T(512)S(1)}, u32[]{:S(2)}) copy-start(f32[384]{0:T(512)S(1)} %get-tuple-element.199) | copy-start | bytes 4612
  88.6 71.3 %copy-start.106 = (f32[1,256]{1,0:T(1,128)}, f32[1,256]{1,0:T(1,128)S(1)}, u32[]{:S(2)}) copy-start(f32[1,256]{1,0:T(1,128)S(1)} %get-tuple-element.279) | copy-start | bytes 3076
  88.6 71.3 %copy-start.108 = (f32[1,256]{1,0:T(1,128)}, f32[1,256]{1,0:T(1,128)S(1)}, u32[]{:S(2)}) copy-start(f32[1,256]{1,0:T(1,128)S(1)} %get-tuple-element.280) | copy-start | bytes 3076
  88.6 71.3 %copy-start.110 = (f32[1,256]{1,0:T(1,128)}, f32[1,256]{1,0:T(1,128)S(1)}, u32[]{:S(2)}) copy-start(f32[1,256]{1,0:T(1,128)S(1)} %get-tuple-element.281) | copy-start | bytes 3076
  88.7 71.3 %copy-start.112 = (f32[1,256]{1,0:T(1,128)}, f32[1,256]{1,0:T(1,128)S(1)}, u32[]{:S(2)}) copy-start(f32[1,256]{1,0:T(1,128)S(1)} %get-tuple-element.282) | copy-start | bytes 3076
  156.2 9.5 %copy-start.6 = (f32[1024,384]{0,1:T(8,128)}, f32[1024,384]{0,1:T(8,128)S(1)}, u32[]{:S(2)}) copy-start(f32[1024,384]{0,1:T(8,128)S(1)} %slice.338) | copy-start | bytes 4718596
  159.6 10.6 %copy-start.80 = (f32[8,6,128]{2,1,0:T(8,128)}, f32[8,6,128]{2,1,0:T(8,128)S(1)}, u32[]{:S(2)}) copy-start(f32[8,6,128]{2,1,0:T(8,128)S(1)} %copy.433) | copy-start | bytes 73732
  164.5 20.1 %copy-start.10 = (bf16[16,8,8,128]{3,2,1,0:T(8,128)(2,1)}, bf16[16,8,8,128]{3,2,1,0:T(8,128)(2,1)S(1)}, u32[]{:S(2)}) copy-start(bf16[16,8,8,128]{3,2,1,0:T(8,128)(2,1)S(1)} %get-tuple-element.260) | copy-start | bytes 786436
  164.8 15.7 %copy-start.70 = (f32[384]{0:T(512)}, f32[384]{0:T(512)S(1)}, u32[]{:S(2)}) copy-start(f32[384]{0:T(512)S(1)} %broadcast_in_dim.207) | copy-start | bytes 4612
  165.0 15.6 %copy-start.68 = (f32[384]{0:T(512)}, f32[384]{0:T(512)S(1)}, u32[]{:S(2)}) copy-start(f32[384]{0:T(512)S(1)} %broadcast_in_dim.210) | copy-start | bytes 4612
  165.1 16.7 %copy-start.58 = (f32[384]{0:T(512)}, f32[384]{0:T(512)S(1)}, u32[]{:S(2)}) copy-start(f32[384]{0:T(512)S(1)} %broadcast_in_dim.212) | copy-start | bytes 4612
  165.3 16.6 %copy-start.60 = (f32[384]{0:T(512)}, f32[384]{0:T(512)S(1)}, u32[]{:S(2)}) copy-start(f32[384]{0:T(512)S(1)} %broadcast_in_dim.214) | copy-start | bytes 4612
  165.4 17.8 %copy-start.72 = (f32[384]{0:T(512)}, f32[384]{0:T(512)S(1)}, u32[]{:S(2)}) copy-start(f32[384]{0:T(512)S(1)} %broadcast_in_dim.216) | copy-start | bytes 4612
  165.6 17.6 %copy-start.74 = (f32[384]{0:T(512)}, f32[384]{0:T(512)S(1)}, u32[]{:S(2)}) copy-start(f32[384]{0:T(512)S(1)} %broadcast_in_dim.218) | copy-start | bytes 4612
  165.8 18.2 %copy-start.78 = (f32[384]{0:T(512)}, f32[384]{0:T(512)S(1)}, u32[]{:S(2)}) copy-start(f32[384]{0:T(512)S(1)} %broadcast_in_dim.220) | copy-start | bytes 4612
  169.7 14.3 %copy-start.3 = (f32[8,128,384]{2,1,0:T(8,128)}, f32[8,128,384]{2,1,0:T(8,128)S(1)}, u32[]{:S(2)}) copy-start(f32[8,128,384]{2,1,0:T(8,128)S(1)} %fusion.82) | copy-start | bytes 4718596
  189.0 11.0 %copy-start.49 = (bf16[1024,128]{0,1:T(8,128)(2,1)S(1)}, bf16[1024,128]{0,1:T(8,128)(2,1)}, u32[]{:S(2)}) copy-start(bf16[1024,128]{0,1:T(8,128)(2,1)} %get-tuple-element.241) | copy-start | bytes 786436
  203.6 8.5 %copy-start.48 = (bf16[1024,128]{0,1:T(8,128)(2,1)S(1)}, bf16[1024,128]{0,1:T(8,128)(2,1)}, u32[]{:S(2)}) copy-start(bf16[1024,128]{0,1:T(8,128)(2,1)} %get-tuple-element.240) | copy-start | bytes 786436
  248.5 56.8 %all-gather.17.cloned.1.call-start = ((), (), s32[]{:S(2)}) async-start(), calls=%async_computation.14 | async-start | bytes 2621440 | tf_op jit(solution)/shard_map/all_gather | solution.py:42
  282.5 47.8 %all-gather.19.cloned.1.call-start = ((), (), s32[]{:S(2)}) async-start(), calls=%async_computation.15 | async-start | bytes 2621440 | tf_op jit(solution)/shard_map/all_gather | solution.py:42
  284.6 88.7 %reduce-scatter.10.cloned.1.call-start = ((), (), s32[]{:S(2)}) async-start(), calls=%async_computation.16 | async-start | bytes 2621440 | tf_op jit(solution)/shard_map/reduce_scatter | solution.py:46
  330.3 7.5 copy-start.133
  341.7 58.3 %all-gather.21.cloned.1.call-start = ((), (), s32[]{:S(2)}) async-start(), calls=%async_computation.17 | async-start | bytes 2621440 | tf_op jit(solution)/shard_map/all_gather | solution.py:42
  377.2 170.9 %reduce-scatter.12.cloned.1.call-start = ((), (), s32[]{:S(2)}) async-start(), calls=%async_computation.18 | async-start | bytes 2621440 | tf_op jit(solution)/shard_map/reduce_scatter | solution.py:46
  399.9 149.4 %reduce-scatter.16.cloned.1.call-start = ((), (), s32[]{:S(2)}) async-start(), calls=%async_computation.20 | async-start | bytes 1310720 | tf_op jit(solution)/shard_map/reduce_scatter | solution.py:52
  430.5 9.2 %copy-start.77 = (f32[1024]{0:T(1024)S(1)}, f32[1024]{0:T(1024)}, u32[]{:S(2)}) copy-start(f32[1024]{0:T(1024)} %copy-done.76) | copy-start | bytes 12292
  454.7 94.7 %reduce-scatter.14.cloned.1.call-start = ((), (), s32[]{:S(2)}) async-start(), calls=%async_computation.19 | async-start | bytes 3932160 | tf_op jit(solution)/shard_map/reduce_scatter | solution.py:52
  454.7 7.7 copy-start.139
  454.7 8.1 %copy-start.45 = (bf16[1024,2,64]{0,1,2:T(2,128)(2,1)S(1)}, bf16[1024,2,64]{0,1,2:T(2,128)(2,1)}, u32[]{:S(2)}) copy-start(bf16[1024,2,64]{0,1,2:T(2,128)(2,1)} %fusion.57) | copy-start | bytes 786436
  480.1 109.3 %reduce-scatter.18.cloned.1.call-start = ((), (), s32[]{:S(2)}) async-start(), calls=%async_computation.21 | async-start | bytes 2621440 | tf_op jit(solution)/shard_map/reduce_scatter | solution.py:46
  539.4 5.5 copy-start.22
  557.0 109.6 %reduce-scatter.20.cloned.1.call-start = ((), (), s32[]{:S(2)}) async-start(), calls=%async_computation.22 | async-start | bytes 3624960 | tf_op jit(solution)/shard_map/reduce_scatter | solution.py:52
  564.2 25.2 %copy-start.67 = (f32[1,1024]{1,0:T(1,128)S(1)}, f32[1,1024]{1,0:T(1,128)}, u32[]{:S(2)}) copy-start(f32[1,1024]{1,0:T(1,128)} %copy-done.66) | copy-start | bytes 12292
  564.2 25.2 %copy-start.105 = (f32[256]{0:T(256)S(1)}, f32[256]{0:T(256)}, u32[]{:S(2)}) copy-start(f32[256]{0:T(256)} %copy-done.104) | copy-start | bytes 3076
  564.2 26.6 %copy-start.117 = (f32[256]{0:T(256)S(1)}, f32[256]{0:T(256)}, u32[]{:S(2)}) copy-start(f32[256]{0:T(256)} %copy-done.116) | copy-start | bytes 3076
  564.2 26.6 %copy-start.18 = (bf16[256,1024]{1,0:T(8,128)(2,1)S(1)}, bf16[256,1024]{1,0:T(8,128)(2,1)}, u32[]{:S(2)}) copy-start(bf16[256,1024]{1,0:T(8,128)(2,1)} %reduce-scatter.10.cloned.1.call-done) | copy-start | bytes 1572868
  564.2 26.6 %copy-start.20 = (bf16[256,1024]{1,0:T(8,128)(2,1)S(1)}, bf16[256,1024]{1,0:T(8,128)(2,1)}, u32[]{:S(2)}) copy-start(bf16[256,1024]{1,0:T(8,128)(2,1)} %copy.458) | copy-start | bytes 1572868
  564.2 26.6 %copy-start.57 = (f32[1,1024]{1,0:T(1,128)S(1)}, f32[1,1024]{1,0:T(1,128)}, u32[]{:S(2)}) copy-start(f32[1,1024]{1,0:T(1,128)} %get-tuple-element.277) | copy-start | bytes 12292
  564.3 26.6 %copy-start.88 = (f32[256]{0:T(256)S(1)}, f32[256]{0:T(256)}, u32[]{:S(2)}) copy-start(f32[256]{0:T(256)} %copy-done.86) | copy-start | bytes 3076
  564.3 26.6 %copy-start.115 = (f32[256]{0:T(256)S(1)}, f32[256]{0:T(256)}, u32[]{:S(2)}) copy-start(f32[256]{0:T(256)} %copy-done.114) | copy-start | bytes 3076
  593.7 74.8 %copy-start.39 = (bf16[256,1536]{0,1:T(8,128)(2,1)S(1)}, bf16[256,1536]{0,1:T(8,128)(2,1)}, u32[]{:S(2)}) copy-start(bf16[256,1536]{0,1:T(8,128)(2,1)} %reduce-scatter.14.cloned.1.call-done) | copy-start | bytes 2359300
  593.7 74.8 %copy-start.50 = (bf16[256,512]{0,1:T(8,128)(2,1)S(1)}, bf16[256,512]{0,1:T(8,128)(2,1)}, u32[]{:S(2)}) copy-start(bf16[256,512]{0,1:T(8,128)(2,1)} %reduce-scatter.16.cloned.1.call-done) | copy-start | bytes 786436
  593.7 135.6 %all-to-all-start.1 = ((bf16[2,256,1024]{1,0,2:T(2,128)(2,1)}), bf16[2,256,1024]{1,0,2:T(2,128)(2,1)S(1)}, u32[]{:S(2)}, u32[]{:S(2)}) async-start(bf16[2,256,1024]{1,0,2:T(2,128)(2,1)} %copy.500), calls=%async_computation.7 | async-start | bytes 2097152 | tf_op jit(solution)/shard_map/all_to_all | solution.py:327
  598.5 128.1 %all-reduce.45.cloned.1.call-start = ((), (), s32[]{:S(2)}) async-start(), calls=%async_computation.23 | async-start | bytes 524288 | tf_op jit(solution)/shard_map/psum | solution.py:337
  668.4 110.8 %all-reduce.47.cloned.1.call-start = ((), (), s32[]{:S(2)}) async-start(), calls=%async_computation.24 | async-start | bytes 3022848 | tf_op jit(solution)/shard_map/psum | solution.py:336
  (100 other events, 230.5 us)
Sparse Core Ops, SparseCore 0:
  61.3 23.7 all-gather.8
  86.7 63.4 all-gather.10
  151.8 62.0 all-gather.12
  215.9 28.3 all-gather.14
  248.6 29.7 reduce-scatter.7
  282.6 22.5 all-gather.16
  307.4 22.8 all-gather.18
  341.8 31.4 reduce-scatter.9
  377.3 22.5 all-gather.20
  402.3 31.4 reduce-scatter.11
  454.8 27.8 reduce-scatter.15
  484.8 58.8 reduce-scatter.13
  557.1 32.2 reduce-scatter.17
  591.7 74.9 reduce-scatter.19
  670.4 56.1 all-reduce.44
  729.5 49.7 all-reduce.46
